TPU v7x, 128 devices: a whole 4x4x4 slice. The times are simulated.
128 devices in a mesh: seq: 16 (over z_lo, x, core), head: 8 (over z_hi, y).
Axes of the slice: x: 4, y: 4, z: 4 (z_hi: 2, z_lo: 2; z = z_hi * 2 + z_lo), core: 2. Of those that a mesh axis runs over, the one named last changes fastest.
Arguments:
- queries: bfloat16 [16384, 2048], P('seq', 'head'), may hold values from -6 to 6
- segment_keys: bfloat16 [16384, 2048], P('seq', 'head'), may hold values from -6 to 6
- segment_values: bfloat16 [16384, 2048], P('seq', 'head'), may hold values from -6 to 6
- memory_keys: bfloat16 [65536, 2048], P('seq', 'head'), may hold values from -8 to 8
- memory_values: bfloat16 [65536, 2048], P('seq', 'head'), may hold values from -6 to 6
- block_index: int32 [64, 8], P('seq'), may hold values from 0 to 1023, as said below
- out_weight: bfloat16 [2048, 4096], P('head'), may hold values from -1.5 to 1.5
Outputs:
- layer_output: bfloat16 [16384, 4096], P('seq', 'head')
Inputs may be any that keep to these rules, and one draw needn't show every extreme that they name: `block_index`: from the groups of one index of seq, one memory shard of 64 blocks (the same shard for every index of seq) receives exactly 8 indices, the same 8 distinct blocks from every index; the remaining indices are spread over the other shards as evenly as possible, in a drawn order, so that each of them receives at most 2 from one index, and some receives exactly 2.
All inputs are finite; a program needn't handle non-finite values.
Results may differ from a plain program's by a relative error of at most 0.019.
Values may be sent and summed in bfloat16 or wider, within the bound.
A program may use at most 128 MiB of HBM per device.

v0:
```python
import math

import jax
import jax.numpy as jnp
from jax import lax
from jax.sharding import PartitionSpec as P

HD = 128
GROUP = 256
BLOCK = 64
TOPB = 8


masked_score = -1e30


def absorb(running, scores, allowed, value_tile):
    run_max, run_sum, run_acc = running
    new_max = jnp.maximum(run_max, jnp.max(jnp.where(allowed, scores, masked_score), axis=-1))
    weights = jnp.where(allowed, jnp.exp(scores - new_max[..., None]), 0.0)
    shrink = jnp.exp(run_max - new_max)
    new_sum = run_sum * shrink + jnp.sum(weights, axis=-1)
    added = jnp.einsum(
        "hqk,khd->hqd", weights.astype(jnp.bfloat16), value_tile, preferred_element_type=jnp.float32
    )
    return (new_max, new_sum, run_acc * shrink[..., None] + added)


def merge_states(first_state, second_state):
    top = jnp.maximum(first_state[0], second_state[0])
    first_factor = jnp.exp(first_state[0] - top)
    second_factor = jnp.exp(second_state[0] - top)
    summed = first_state[1] * first_factor + second_state[1] * second_factor
    joined = first_state[2] * first_factor[..., None] + second_state[2] * second_factor[..., None]
    return (top, summed, joined)


def slot_places(member, local_block, width):
    earlier = jnp.cumsum(member, axis=0) - member
    position = jnp.sum(earlier * member, axis=1)
    placed = member[:, :, None] * (
        position[:, None, None] == jnp.arange(width, dtype=jnp.int32)[None, None, :]
    ).astype(jnp.int32)
    requests = jnp.sum(placed * local_block[:, None, None], axis=0)
    return (position, requests)


def fetch_memory(block_index, memory_keys, memory_values, heads_local):
    owners_n = lax.axis_size("seq")
    block_rows = memory_keys.shape[0] // BLOCK
    row_width = memory_keys.shape[1]
    wanted = block_index.reshape(-1)
    slot_count = wanted.shape[0]
    capacity = slot_count // 4
    holder = wanted // block_rows
    local_block = wanted - holder * block_rows
    owner_ids = jnp.arange(owners_n, dtype=jnp.int32)
    member = (holder[:, None] == owner_ids[None, :]).astype(jnp.int32)
    key_table = memory_keys.reshape(block_rows, BLOCK, row_width)
    value_table = memory_values.reshape(block_rows, BLOCK, row_width)
    position, requests = slot_places(member, local_block, capacity)
    incoming = lax.all_to_all(requests, "seq", split_axis=0, concat_axis=0, tiled=True)
    flat_in = incoming.reshape(-1)
    key_blocks = jnp.take(key_table, flat_in, axis=0).reshape(owners_n, capacity, BLOCK, row_width)
    value_blocks = jnp.take(value_table, flat_in, axis=0).reshape(
        owners_n, capacity, BLOCK, row_width
    )
    got_keys, got_values = (
        lax.all_to_all(key_blocks, "seq", split_axis=0, concat_axis=0, tiled=True),
        lax.all_to_all(value_blocks, "seq", split_axis=0, concat_axis=0, tiled=True),
    )
    all_keys = got_keys.reshape(owners_n * capacity, BLOCK, row_width)
    all_values = got_values.reshape(owners_n * capacity, BLOCK, row_width)
    slot_index = holder * capacity + position
    group_count = block_index.shape[0]
    fetched_keys = jnp.take(all_keys, slot_index, axis=0).reshape(
        group_count, TOPB * BLOCK, heads_local, HD
    )
    fetched_values = jnp.take(all_values, slot_index, axis=0).reshape(
        group_count, TOPB * BLOCK, heads_local, HD
    )
    return (fetched_keys, fetched_values)


def shards(
    queries, segment_keys, segment_values, memory_keys, memory_values, block_index, out_weight
):
    tok_rows = queries.shape[0]
    heads_local = queries.shape[1] // HD
    group_count = block_index.shape[0]
    score_scale = HD ** (-0.5)
    query_heads = queries.reshape(tok_rows, heads_local, HD)
    first_row = lax.axis_index("seq") * tok_rows
    query_pos = first_row + jnp.arange(tok_rows, dtype=jnp.int32)
    last_row = first_row + tok_rows - 1
    initial = (
        jnp.full((heads_local, tok_rows), masked_score, jnp.float32),
        jnp.zeros((heads_local, tok_rows), jnp.float32),
        jnp.zeros((heads_local, tok_rows, HD), jnp.float32),
    )
    key_part = lax.all_gather(segment_keys, "seq", axis=0, tiled=True)
    value_part = lax.all_gather(segment_values, "seq", axis=0, tiled=True)
    count_rows = key_part.shape[0]
    tile_rows = math.gcd(count_rows, 1024)
    tile_count = count_rows // tile_rows
    key_tiles = key_part.reshape(tile_count, tile_rows, heads_local, HD)
    value_tiles = value_part.reshape(tile_count, tile_rows, heads_local, HD)
    tile_starts = tile_rows * jnp.arange(tile_count, dtype=jnp.int32)

    def visit_tile(current, element):
        key_tile, value_tile, tile_start = element

        def update(inner):
            scores = (
                jnp.einsum(
                    "qhd,khd->hqk", query_heads, key_tile, preferred_element_type=jnp.float32
                )
                * score_scale
            )
            allowed = (tile_start + jnp.arange(tile_rows, dtype=jnp.int32))[None, :] <= query_pos[
                :, None
            ]
            return absorb(inner, scores, allowed[None], value_tile)

        def unchanged(inner):
            return inner

        return (lax.cond(tile_start <= last_row, update, unchanged, current), None)

    result, _ = lax.scan(visit_tile, initial, (key_tiles, value_tiles, tile_starts))
    fetched_keys, fetched_values = fetch_memory(
        block_index, memory_keys, memory_values, heads_local
    )
    query_groups = queries.reshape(group_count, GROUP, heads_local, HD)
    scores = (
        jnp.einsum(
            "cqhd,ckhd->chqk", query_groups, fetched_keys, preferred_element_type=jnp.float32
        )
        * score_scale
    )
    group_max = jnp.max(scores, axis=-1)
    weights = jnp.exp(scores - group_max[..., None])
    group_sum = jnp.sum(weights, axis=-1)
    group_acc = jnp.einsum(
        "chqk,ckhd->chqd",
        weights.astype(jnp.bfloat16),
        fetched_values,
        preferred_element_type=jnp.float32,
    )
    mem_max = jnp.transpose(group_max, (1, 0, 2)).reshape(heads_local, tok_rows)
    mem_sum = jnp.transpose(group_sum, (1, 0, 2)).reshape(heads_local, tok_rows)
    mem_acc = jnp.transpose(group_acc, (1, 0, 2, 3)).reshape(heads_local, tok_rows, HD)
    final_state = merge_states(result, (mem_max, mem_sum, mem_acc))
    run_max, run_sum, run_acc = final_state
    attended = (
        (run_acc / run_sum[..., None])
        .transpose(1, 0, 2)
        .reshape(tok_rows, heads_local * HD)
        .astype(jnp.bfloat16)
    )
    partial_value = jnp.dot(attended, out_weight, preferred_element_type=jnp.float32)
    combined = lax.psum_scatter(
        partial_value.astype(jnp.bfloat16), "head", scatter_dimension=1, tiled=True
    )
    return combined


def solution(mesh):
    in_specs = (
        P("seq", "head"),
        P("seq", "head"),
        P("seq", "head"),
        P("seq", "head"),
        P("seq", "head"),
        P("seq", None),
        P("head", None),
    )
    out_specs = P("seq", "head")
    return jax.shard_map(shards, mesh=mesh, in_specs=in_specs, out_specs=out_specs, check_vma=False)
```

profile of v0, /device:TPU:0, one launch (start us, length us, event | category | flops | bytes accessed | tf_op | source)
XLA Modules:
  0.0 581.3 jit_solution(2751178568303068386)
XLA Ops:
  8.0 0.8 reshape.212
  9.5 11.7 %all_to_all.19 = s32[16,1,8]{2,1,0:T(1,128)S(1)} all-to-all(s32[16,1,8]{2,1,0:T(1,128)S(1)} %bitcast.80), channel_id=1, replica_groups=mesh['seq'=16,'head'=8] {'seq'}, dimensions={0} | all-to-all | bytes 1024 | tf_op jit(solution)/shard_map/all_to_all | solution.py:62
  22.5 4.4 gather_fusion.2
  26.9 4.3 gather_fusion
  31.2 5.5 broadcast_select_fusion
  36.7 70.9 %all_to_all.20 = bf16[16,8,64,256]{3,2,1,0:T(8,128)(2,1)} all-to-all(bf16[16,8,64,256]{3,2,1,0:T(8,128)(2,1)S(1)} %bitcast.71), channel_id=1, replica_groups=mesh['seq'=16,'head'=8] {'seq'}, dimensions={0} | all-to-all | bytes 8388608 | tf_op jit(solution)/shard_map/all_to_all | solution.py:69
  107.6 4.7 all-to-all-start.2
  112.3 1.0 reshape.217
  113.5 1.0 copy.45
  114.6 2.8 gather_fusion.1
  117.4 64.2 %all-to-all-done.2 = bf16[16,8,64,256]{3,2,1,0:T(8,128)(2,1)} async-done(((bf16[16,8,64,256]{3,2,1,0:T(8,128)(2,1)}), bf16[16,8,64,256]{3,2,1,0:T(8,128)(2,1)}, u32[]{:S(2)}, u32[]{:S(2)}) %all-to-all-start.2) | async-done | bytes 4194336 | tf_op jit(solution)/shard_map/all_to_all | solution.py:70
  181.5 3.9 gather_fusion.3
  185.4 2.8 broadcast_select_fusion.2
  188.2 1.3 reshape.222
  189.6 2.1 reshape.216
  191.7 2.1 bitcast_reduce_fusion
  193.8 1.1 fusion.29
  195.8 12.6 %reshape.269 = bf16[16,1024,2,128]{3,2,1,0:T(2,128)(2,1)} reshape(bf16[16384,256]{1,0:T(8,128)(2,1)} %all-gather.3.cloned.1.call-done) | data formatting | bytes 16777216 | tf_op jit(solution)/shard_map/reshape | solution.py:106
  208.4 8.6 %copy.44 = bf16[16,1024,2,128]{3,1,2,0:T(8,128)(2,1)} copy(bf16[16,1024,2,128]{3,2,1,0:T(2,128)(2,1)} %reshape.269) | data formatting | bytes 16777216
  217.0 12.5 %reshape.270 = bf16[16,1024,2,128]{3,2,1,0:T(2,128)(2,1)} reshape(bf16[16384,256]{1,0:T(8,128)(2,1)} %all-gather.5.cloned.1.call-done) | data formatting | bytes 16777216 | tf_op jit(solution)/shard_map/reshape | solution.py:107
  229.5 8.6 %copy.46 = bf16[16,1024,2,128]{3,1,2,0:T(8,128)(2,1)} copy(bf16[16,1024,2,128]{3,2,1,0:T(2,128)(2,1)} %reshape.270) | data formatting | bytes 16777216
  238.1 1.0 broadcast_in_dim.69
  239.2 31.9 %while.15 = (s32[]{:T(128)}, f32[2,1024]{1,0:T(2,128)S(1)}, f32[2,1024]{1,0:T(2,128)S(1)}, f32[2,1024,128]{2,1,0:T(8,128)}, s32[16]{0:T(128)S(1)}, /*index=5*/s3...) while((s32[]{:T(128)}, f32[2,1024]{1,0:T(2,128)S(1)}, ...), condition=%wide.region_5.6_spmd.clone, body=%wide.region_0.5_spmd.clone.sunk | while | flops 1098389504 | bytes 41575768 | solution.py:130
  240.4 11.7 %conditional.3 = ((f32[2,1024]{1,0:T(2,128)S(1)}, f32[2,1024]{1,0:T(2,128)S(1)}, f32[2,1024,128]{2,1,0:T(8,128)})) conditional(s32[]{:T(128)} %convert_element_type.61, (f32[2,1024]{1,0:T(2,128)S(1)}, f32[2,1024]{1,0:T(2,128)S(1)}, f32[2,1024,128]{2,1,0:T(8,128)}) %tuple.51, (s32[]{:T(128)}, s32[]{:T(128)}, bf16[16,1024,2,128]{3,1,2,0:T(8,128)(2,1)}, ...), branch_computations={%region_1.1_spmd, %region_2.4_spmd} | conditional | flops 1098389504 | bytes 41571424 | solution.py:128
  241.7 3.0 fusion.2
  244.7 2.0 fusion.6
  246.8 4.3 fusion.10
  251.1 1.0 copy-done.2
  271.1 2.7 fusion.34
  273.8 1.2 copy.55
  275.1 5.6 convolution_convert_fusion
  280.7 294.1 %reduce-scatter.2.cloned.1.call-done = bf16[1024,512]{1,0:T(8,128)(2,1)} async-done(((bf16[1024,4096]{1,0:T(8,128)(2,1)}), bf16[1024,512]{1,0:T(8,128)(2,1)}) %reduce-scatter.2.cloned.1.call-update) | async-done | bytes 1048592 | tf_op jit(solution)/shard_map/reduce_scatter | solution.py:162
  (89 shorter events, 15.7 us)
Async XLA Ops:
  6.5 268.6 %copy-start = (bf16[256,4096]{1,0:T(8,128)(2,1)S(1)}, bf16[256,4096]{1,0:T(8,128)(2,1)}, u32[]{:S(2)}) copy-start(bf16[256,4096]{1,0:T(8,128)(2,1)} %param.21) | copy-start | bytes 6291460
  6.5 189.2 %all-gather.3.cloned.1.call-start = ((), (), s32[]{:S(2)}) async-start(), calls=%async_computation.4 | async-start | bytes 8912896 | tf_op jit(solution)/shard_map/all_gather | solution.py:101
  7.3 209.7 %all-gather.5.cloned.1.call-start = ((), (), s32[]{:S(2)}) async-start(), calls=%async_computation.5 | async-start | bytes 8912896 | tf_op jit(solution)/shard_map/all_gather | solution.py:102
  107.6 4.7 copy-start.3
  107.6 73.9 %all-to-all-start.2 = ((bf16[16,8,64,256]{3,2,1,0:T(8,128)(2,1)}), bf16[16,8,64,256]{3,2,1,0:T(8,128)(2,1)}, u32[]{:S(2)}, u32[]{:S(2)}) async-start(bf16[16,8,64,256]{3,2,1,0:T(8,128)(2,1)} %bitcast.70), calls=%async_computation.2 | async-start | bytes 8388608 | tf_op jit(solution)/shard_map/all_to_all | solution.py:70
  112.3 462.5 %reduce-scatter.2.cloned.1.call-start = ((), (), s32[]{:S(2)}) async-start(), calls=%async_computation.6 | async-start | bytes 9437184 | tf_op jit(solution)/shard_map/reduce_scatter | solution.py:162
  244.7 2.0 copy-start.1
  251.1 1.0 copy-start.2
Sparse Core Ops, SparseCore 0:
  9.1 98.1 all-gather.2
  109.0 93.4 all-gather.4
  280.8 293.9 reduce-scatter.1
where the time goes:
time: 584 us; the launch traced here: 581 us
  waiting for transfers between devices  360 us (62%)
  blocking collectives  82.6 us (14%)
  local copies, waits for them, and re-layouts  77.7 us (13%)
  other arithmetic  16.4 us (3%)
  matrix products  16.2 us (3%)
  between operations  13.3 us (2%)
  loops' own time  10.8 us (2%)
    reduce_scatter x1, waiting for transfers between devices, shards(): lax.psum_scatter(partial_value.astype(jnp.bfloat16), 'head', scatter_dime...  294 us
    all_to_all x1, blocking collectives, fetch_memory(): lax.all_to_all(key_blocks, 'seq', split_axis=0, concat_axis=0, tiled=True)  70.9 us
    all_to_all x1, waiting for transfers between devices, fetch_memory(): lax.all_to_all(value_blocks, 'seq', split_axis=0, concat_axis=0, tiled=True)  64.2 us
    unnamed x8, local copies, waits for them, and re-layouts  18.5 us
    reshape x1, local copies, waits for them, and re-layouts, shards(): key_tiles = key_part.reshape(tile_count, tile_rows, heads_local, HD)  12.6 us
    reshape x1, local copies, waits for them, and re-layouts, shards(): value_tiles = value_part.reshape(tile_count, tile_rows, heads_local, HD)  12.5 us
    all_to_all x1, blocking collectives, fetch_memory(): lax.all_to_all(requests, 'seq', split_axis=0, concat_axis=0, tiled=True)  11.7 us
  transfers between devices with their start and end apart: 4, of which 2 were waited for; matrix products, arithmetic and copies ran while one was open for 10% of the time, Pallas kernels for 0%

commit v1 on v0

v1 whole, which is shorter than its diff:
```python
import functools
import math

import jax
import jax.numpy as jnp
from jax import lax
from jax.experimental import pallas as pl
from jax.experimental.pallas import tpu as pltpu
from jax.sharding import PartitionSpec as P

MESH = pl.DeviceIdType.MESH
HD = 128
GROUP = 256
BLOCK = 64
TOPB = 8
ROWS = 1024
CHUNK = 256
SCALE = math.log2(math.e) / math.sqrt(HD)
LOW = -1e30
STEPS = 24


def where_am_i():
    s = lax.axis_index("seq")
    hd = lax.axis_index("head")
    return s, hd, s // 8, (s // 2) % 4, s % 2, hd // 4, hd % 4


def seq_of(z, x, c):
    return z * 8 + x * 2 + c


def dot_nt(a, b):
    return lax.dot_general(a, b, (((1,), (1,)), ((), ())), preferred_element_type=jnp.float32)


def pick(t, table, default):
    out = default
    for k, v in table.items():
        out = jnp.where(t == k, v, out)
    return out


def remote(src, dst, ss, rs, dev):
    return pltpu.make_async_remote_copy(
        src_ref=src, dst_ref=dst, send_sem=ss, recv_sem=rs, device_id=dev, device_id_type=MESH
    )


DXS = (0, 0, 3, 1, 3, 1, 2, 2)
SIBS = (0, 1, 0, 0, 1, 1, 0, 1)
SERVICE_A = {1: 1, 2: 2, 4: 4, 5: 5, 6: 8, 7: 7, 10: 9, 12: 10, 16: 12, 18: 13, 20: 14, 22: 15}
SERVICE_B = {2: 3, 6: 6, 12: 11}


def attention_kernel(
    q_hbm, k_hbm, v_hbm, mk_hbm, mv_hbm, req_ref, info_ref, w_hbm,
    o_ref, wc_hbm,
    q, kv, m_s, l_s, acc, mk, mv, stage, mem, kc, vc,
    hsend, hown, hr0, hm1, hr1, hm2, hr2, hm3, hr3,
    reqin, infoin, reqs, infos,
    loc_sem, kv_recv, ring_send, swap_send, q_recv, info_recv,
    req_send, req_recv, mem_send, mem_recv, hot_send, hot_recv, w_send, w_recv,
):
    s, hd, z, x, c, zh, y = where_am_i()
    me = s
    zp = seq_of(1 - z, x, c)
    sib = seq_of(z, x, 1 - c)
    xr = seq_of(z, lax.rem(x + 1, 4), c)
    xl = seq_of(z, lax.rem(x + 3, 4), c)

    mine = pl.ds(pl.multiple_of(z * HD, HD), HD)
    theirs = pl.ds(pl.multiple_of((1 - z) * HD, HD), HD)
    loc = [
        pltpu.make_async_copy(k_hbm.at[:, mine], kv.at[s, 0], loc_sem.at[0]),
        pltpu.make_async_copy(v_hbm.at[:, mine], kv.at[s, 1], loc_sem.at[1]),
        pltpu.make_async_copy(q_hbm.at[:, mine], q.at[z], loc_sem.at[2]),
        pltpu.make_async_copy(mk_hbm, mk, loc_sem.at[3]),
        pltpu.make_async_copy(mv_hbm, mv, loc_sem.at[4]),
        pltpu.make_async_copy(info_ref, infos.at[z], loc_sem.at[5]),
        pltpu.make_async_copy(req_ref.at[s], reqin.at[s], loc_sem.at[6]),
    ]
    for cp in loc:
        cp.start()

    bar = pltpu.get_barrier_semaphore()

    def w_target(i):
        same = (i // 4) == zh
        zd = jnp.where(same, z, 1 - z)
        return (seq_of(zd, x, c), i)

    def greet(i, _):
        @pl.when(i != s)
        def _():
            pl.semaphore_signal(bar, inc=1, device_id=(i, hd), device_id_type=MESH)
        return 0

    lax.fori_loop(0, 16, greet, 0)

    def greet_w(i, _):
        @pl.when(i != hd)
        def _():
            pl.semaphore_signal(bar, inc=1, device_id=w_target(i), device_id_type=MESH)
        return 0

    lax.fori_loop(0, 8, greet_w, 0)
    pl.semaphore_wait(bar, 22)

    swaps = [
        remote(k_hbm.at[:, theirs], kv.at[s, 0], swap_send.at[0], kv_recv.at[s * 2], (zp, hd)),
        remote(v_hbm.at[:, theirs], kv.at[s, 1], swap_send.at[1], kv_recv.at[s * 2 + 1], (zp, hd)),
        remote(info_ref, infoin, swap_send.at[2], info_recv.at[0], (zp, hd)),
        remote(q_hbm.at[:, theirs], q.at[z], swap_send.at[3], q_recv.at[0], (zp, hd)),
    ]
    for cp in swaps:
        cp.start()

    def req_copy(i):
        return remote(req_ref.at[i], reqin.at[s], req_send.at[i], req_recv.at[s], (i, hd))

    def send_req(i, _):
        @pl.when(i != s)
        def _():
            req_copy(i).start()
        return 0

    lax.fori_loop(0, 16, send_req, 0)

    loc[0].wait()
    loc[1].wait()

    def ring_copy(half, n, g, k, dev):
        return remote(
            kv.at[g, k], kv.at[g, k], ring_send.at[half * 14 + n], kv_recv.at[g * 2 + k], (dev, hd)
        )

    def sends_of(kind, half, g):
        if kind == 0:
            return [
                ring_copy(half, 0, g, 0, xr), ring_copy(half, 1, g, 0, xl),
                ring_copy(half, 2, g, 1, xr), ring_copy(half, 3, g, 1, xl),
                ring_copy(half, 4, g, 0, sib), ring_copy(half, 5, g, 1, sib),
            ]
        if kind == 2:
            return [
                ring_copy(half, 6, g, 0, xr),
                ring_copy(half, 7, g, 0, sib), ring_copy(half, 8, g, 1, sib),
            ]
        if kind == 3:
            return [
                ring_copy(half, 9, g, 1, xl),
                ring_copy(half, 10, g, 0, sib), ring_copy(half, 11, g, 1, sib),
            ]
        return [ring_copy(half, 12, g, 0, sib), ring_copy(half, 13, g, 1, sib)]

    def block_of(half, i):
        dx = pick(i, dict(enumerate(DXS)), 0)
        sb = pick(i, dict(enumerate(SIBS)), 0)
        return seq_of(half, lax.rem(x + dx, 4), jnp.where(sb == 1, 1 - c, c))

    for cp in sends_of(0, z, s):
        cp.start()

    def w_copy(i):
        cols = pl.ds(pl.multiple_of(i * 512, 512), 512)
        rows = pl.ds(pl.multiple_of(hd * 256, 256), 256)
        return remote(
            w_hbm.at[:, cols], wc_hbm.at[rows, :], w_send.at[i], w_recv.at[hd], w_target(i)
        )

    def send_w(i, _):
        @pl.when(i != hd)
        def _():
            w_copy(i).start()
        return 0

    lax.fori_loop(0, 8, send_w, 0)
    w_local = pltpu.make_async_copy(
        w_hbm.at[:, pl.ds(pl.multiple_of(hd * 512, 512), 512)],
        wc_hbm.at[pl.ds(pl.multiple_of(hd * 256, 256), 256), :],
        loc_sem.at[7],
    )
    w_local.start()

    m_s[...] = jnp.full_like(m_s, LOW)
    l_s[...] = jnp.zeros_like(l_s)
    acc[...] = jnp.zeros_like(acc)

    def wait_block(g):
        for k in range(2):
            remote(kv.at[g, k], kv.at[g, k], ring_send.at[0], kv_recv.at[g * 2 + k], (sib, hd)).wait_recv()

    def service(code):
        @pl.when(code >= 0)
        def _():
            half = jnp.where(code >= 8, 1 - z, z)
            i = lax.rem(code, 8)
            g = block_of(half, i)
            wait_block(g)
            for kind in (0, 2, 3, 6):
                @pl.when(i == kind)
                def _(kind=kind):
                    for cp in sends_of(kind, half, g):
                        cp.start()

    def pipelined(n, scores, finish):
        state = scores(0)
        for j in range(n):
            later = scores(j + 1) if j + 1 < n else None
            finish(j, state)
            state = later

    def absorb(qh, rows, sc, val):
        mo = m_s[qh, rows, :]
        mn = jnp.maximum(mo, jnp.max(sc, axis=-1, keepdims=True))
        m_s[qh, rows, :] = mn
        return sc, mo, mn, val

    def settle(qh, rows, state):
        sc, mo, mn, val = state
        p = jnp.exp2((sc - mn[:, :1]) * SCALE)
        sh = jnp.exp2((mo - mn) * SCALE)
        ls = p[:, 0:128]
        for u in range(1, p.shape[1] // 128):
            ls = ls + p[:, u * 128:(u + 1) * 128]
        l_s[qh, rows, :] = l_s[qh, rows, :] * sh + ls
        acc[qh, rows, :] = acc[qh, rows, :] * sh + jnp.dot(
            p.astype(jnp.bfloat16), val(), preferred_element_type=jnp.float32
        )

    def attend(qh, g):
        gq = seq_of(qh, x, c)

        @pl.when(g < gq)
        def _():
            def scores(j):
                rows = pl.ds(j * CHUNK, CHUNK)
                return absorb(
                    qh, rows, dot_nt(q[qh, rows, :], kv[g, 0, :, :]), lambda: kv[g, 1, :, :]
                )

            pipelined(ROWS // CHUNK, scores, lambda j, st: settle(qh, pl.ds(j * CHUNK, CHUNK), st))

        @pl.when(g == gq)
        def _():
            def scores(j):
                rows = pl.ds(j * CHUNK, CHUNK)
                n = (j + 1) * CHUNK
                sc = dot_nt(q[qh, rows, :], kv[g, 0, 0:n, :])
                last = sc[:, n - CHUNK:]
                ok = lax.broadcasted_iota(jnp.int32, (CHUNK, CHUNK), 1) <= lax.broadcasted_iota(
                    jnp.int32, (CHUNK, CHUNK), 0
                )
                last = jnp.where(ok, last, LOW)
                if j:
                    last = jnp.concatenate([sc[:, : n - CHUNK], last], axis=1)
                return absorb(qh, rows, last, lambda: kv[g, 1, 0:n, :])

            pipelined(ROWS // CHUNK, scores, lambda j, st: settle(qh, pl.ds(j * CHUNK, CHUNK), st))

    def mem_copy(r, e):
        dst = seq_of(e, (r // 2) % 4, lax.rem(r, 2))
        at = (r // 8) * 16 + s
        return dst, at

    def pair(at):
        return mem.at[pl.ds(at * 2, 2)]

    def mem_remote(r, e):
        dst, at = mem_copy(r, e)
        return remote(
            stage.at[r, e], pair(at), mem_send.at[r * 2 + e], mem_recv.at[at], (dst, hd)
        )

    def hot_copy(n, src, dst, dev):
        return remote(src, dst, hot_send.at[n], hot_recv.at[n], (dev, hd))

    hx1 = seq_of(z, jnp.where(x % 2 == 0, x + 1, x - 1), c)
    hx2 = seq_of(z, 3 - x, c)

    def hot_copies(n):
        if n == 0:
            return hot_copy(0, hsend, hr0, sib)
        if n == 1:
            return hot_copy(1, hm1.at[1 - z], hr1, zp)
        if n == 2:
            return hot_copy(2, hm2, hr2, hx1)
        if n == 3:
            return hot_copy(3, hm3, hr3, hx2)
        return hot_copy(4, mem.at[pl.ds(64, 8), c], mem.at[pl.ds(64, 8), c], sib)

    def hot_owner():
        return infos[z, 0, 40]

    def step(t, _):
        @pl.when(t == 8)
        def _():
            remote(q.at[0], q.at[1 - z], swap_send.at[3], q_recv.at[0], (zp, hd)).wait_recv()

        service(pick(t, SERVICE_A, -1))
        service(pick(t, SERVICE_B, -1))

        @pl.when(t == 1)
        def _():
            def wait_req(i, _):
                @pl.when(i != s)
                def _():
                    remote(
                        req_ref.at[i], reqin.at[i], req_send.at[i], req_recv.at[i], (sib, hd)
                    ).wait_recv()
                return 0

            lax.fori_loop(0, 16, wait_req, 0)
            swaps[2].wait_recv()
            for cp in loc[3:]:
                cp.wait()
            a = pltpu.make_async_copy(reqin, reqs, loc_sem.at[8])
            b = pltpu.make_async_copy(infoin, infos.at[1 - z], loc_sem.at[9])
            a.start()
            b.start()
            a.wait()
            b.wait()

            def hot_rows(j, _):
                b = infos[z, 0, 32 + j]
                kr = mk[b]
                vr = mv[b]
                for e in range(2):
                    cols = slice(e * HD, (e + 1) * HD)
                    hown[e, j] = jnp.where(c == 0, kr[:, cols], vr[:, cols])
                    hsend[e, j] = jnp.where(c == 0, vr[:, cols], kr[:, cols])
                return 0

            lax.fori_loop(0, 8, hot_rows, 0)
            hot_copies(0).start()

            def gather(r, _):
                for b2 in range(2):
                    b = reqs[r, 0, b2]
                    kr = mk[b]
                    vr = mv[b]
                    for e in range(2):
                        cols = slice(e * HD, (e + 1) * HD)
                        stage[r, e, b2, 0] = kr[:, cols]
                        stage[r, e, b2, 1] = vr[:, cols]
                return 0

            lax.fori_loop(0, 16, gather, 0)

        @pl.when(t == 4)
        def _():
            hot_copies(0).wait_recv()
            keep = hot_owner() == me
            hm1[...] = jnp.where(keep, hown[...], hr0[...])
            hot_copies(1).start()

        @pl.when(t == 6)
        def _():
            def send(i, _):
                r = lax.rem(i // 2 + s + 1, 16)
                e = lax.rem(i, 2)
                dst, at = mem_copy(r, e)

                @pl.when(dst == s)
                def _():
                    pltpu.make_async_copy(stage.at[r, e], pair(at), mem_recv.at[at]).start()

                @pl.when(dst != s)
                def _():
                    mem_remote(r, e).start()
                return 0

            lax.fori_loop(0, 32, send, 0)

        @pl.when(t == 7)
        def _():
            hot_copies(1).wait_recv()
            keep = (hot_owner() // 8) == z
            hm2[...] = jnp.where(keep, hm1[z], hr1[...])
            hot_copies(2).start()

        @pl.when(t == 11)
        def _():
            hot_copies(2).wait_recv()
            keep = ((hot_owner() // 2) % 4) == x
            hm3[...] = jnp.where(keep, hm2[...], hr2[...])
            hot_copies(3).start()

        @pl.when(t == 14)
        def _():
            hot_copies(3).wait_recv()
            keep = ((hot_owner() // 4) % 2) == (x // 2)
            for j in range(8):
                mem[64 + j, c] = jnp.where(keep, hm3[j], hr3[j])
            hot_copies(4).start()

        native = t < 8
        u = t - 8
        qh = jnp.where(native, z, jnp.where(z == 0, 1, lax.rem(t, 2)))
        half = jnp.where(native, z, jnp.where((z == 0) & (u >= 8), 1, 0))
        i = jnp.where(native, t, jnp.where(z == 0, lax.rem(t, 8), u // 2))
        attend(qh, block_of(half, i))
        return 0

    loc[2].wait()
    lax.fori_loop(0, STEPS, step, 0)

    def wait_mem(i, _):
        o = lax.rem(i, 16)

        @pl.when(o != s)
        def _():
            remote(stage.at[0, 0], pair(i), mem_send.at[0], mem_recv.at[i], (sib, hd)).wait_recv()

        @pl.when(o == s)
        def _():
            pltpu.make_async_copy(stage.at[0, 0], pair(i), mem_recv.at[i]).wait()
        return 0

    lax.fori_loop(0, 32, wait_mem, 0)
    remote(
        mem.at[pl.ds(64, 8), 0], mem.at[pl.ds(64, 8), 1 - c], hot_send.at[4], hot_recv.at[4], (sib, hd)
    ).wait_recv()

    def mem_group(i, _):
        qh = i // 4
        j = lax.rem(i, 4)
        for e in range(TOPB):
            code = infos[qh, 0, j * TOPB + e]
            kc[e * BLOCK:(e + 1) * BLOCK, :] = mem[code, 0]
            vc[e * BLOCK:(e + 1) * BLOCK, :] = mem[code, 1]
        rows = pl.ds(pl.multiple_of(j * GROUP, GROUP), GROUP)
        st = absorb(qh, rows, dot_nt(q[qh, rows, :], kc[...]), lambda: vc[...])
        settle(qh, rows, st)
        o_ref[qh, rows, :] = (
            acc[qh, rows, :] / jnp.sum(l_s[qh, rows, :], axis=-1, keepdims=True)
        ).astype(jnp.bfloat16)
        return 0

    lax.fori_loop(0, 8, mem_group, 0)

    for cp in swaps:
        cp.wait_send()
    for half in (0, 1):
        for kind in (0, 2, 3, 6):
            for cp in sends_of(kind, half, s):
                cp.wait_send()
    for n in range(5):
        hot_copies(n).wait_send()

    def drain_req(i, _):
        @pl.when(i != s)
        def _():
            req_copy(i).wait_send()
        return 0

    lax.fori_loop(0, 16, drain_req, 0)

    def drain_mem(i, _):
        dst, _at = mem_copy(i // 2, lax.rem(i, 2))

        @pl.when(dst != s)
        def _():
            mem_remote(i // 2, lax.rem(i, 2)).wait_send()
        return 0

    lax.fori_loop(0, 32, drain_mem, 0)

    def drain_w(i, _):
        @pl.when(i != hd)
        def _():
            w_copy(i).wait_send()
            rows = pl.ds(pl.multiple_of(i * 256, 256), 256)
            remote(
                w_hbm.at[:, pl.ds(0, 512)], wc_hbm.at[rows, :], w_send.at[i], w_recv.at[i], (sib, hd)
            ).wait_recv()
        return 0

    lax.fori_loop(0, 8, drain_w, 0)
    w_local.wait()


def attention(q, k, v, mk, mv, req, info, w):
    any_ = pl.BlockSpec(memory_space=pl.ANY)
    vm = pl.BlockSpec(memory_space=pltpu.VMEM)
    b16 = jnp.bfloat16
    hot = (8, BLOCK, HD)
    dma = pltpu.SemaphoreType.DMA
    return pl.pallas_call(
        attention_kernel,
        out_shape=(
            jax.ShapeDtypeStruct((2, ROWS, HD), b16),
            jax.ShapeDtypeStruct((2048, 512), b16),
        ),
        in_specs=[any_] * 5 + [vm, vm, any_],
        out_specs=(vm, any_),
        scratch_shapes=[
            pltpu.VMEM((2, ROWS, HD), b16),
            pltpu.VMEM((16, 2, ROWS, HD), b16),
            pltpu.VMEM((2, ROWS, HD), jnp.float32),
            pltpu.VMEM((2, ROWS, HD), jnp.float32),
            pltpu.VMEM((2, ROWS, HD), jnp.float32),
            pltpu.VMEM((64, BLOCK, 2 * HD), b16),
            pltpu.VMEM((64, BLOCK, 2 * HD), b16),
            pltpu.VMEM((16, 2, 2, 2, BLOCK, HD), b16),
            pltpu.VMEM((72, 2, BLOCK, HD), b16),
            pltpu.VMEM((TOPB * BLOCK, HD), b16),
            pltpu.VMEM((TOPB * BLOCK, HD), b16),
            pltpu.VMEM((2,) + hot, b16),
            pltpu.VMEM((2,) + hot, b16),
            pltpu.VMEM((2,) + hot, b16),
            pltpu.VMEM((2,) + hot, b16),
            pltpu.VMEM(hot, b16),
            pltpu.VMEM(hot, b16),
            pltpu.VMEM(hot, b16),
            pltpu.VMEM(hot, b16),
            pltpu.VMEM(hot, b16),
            pltpu.VMEM((16, 8, 128), jnp.int32),
            pltpu.VMEM((8, 128), jnp.int32),
            pltpu.SMEM((16, 8, 128), jnp.int32),
            pltpu.SMEM((2, 8, 128), jnp.int32),
            dma((10,)),
            dma((32,)),
            dma((28,)),
            dma((4,)),
            dma((1,)),
            dma((1,)),
            dma((16,)),
            dma((16,)),
            dma((32,)),
            dma((32,)),
            dma((5,)),
            dma((5,)),
            dma((8,)),
            dma((8,)),
        ],
        compiler_params=pltpu.CompilerParams(
            collective_id=0, has_side_effects=True, vmem_limit_bytes=56 << 20
        ),
        name="attention",
    )(q, k, v, mk, mv, req, info, w)


def gather_kernel(o_ref, a_ref, send, recv, ysend, yrecv, loc_sem):
    s, hd, z, x, c, zh, y = where_am_i()
    up = zh * 4 + lax.rem(y + 1, 4)
    dn = zh * 4 + lax.rem(y + 3, 4)
    peers = [(1 - z, zh), (1 - z, 1 - zh), (z, 1 - zh)]
    bar = pltpu.get_barrier_semaphore()
    for zd, zhd in peers:
        pl.semaphore_signal(
            bar, inc=1, device_id=(seq_of(zd, x, c), zhd * 4 + y), device_id_type=MESH
        )
    pl.semaphore_signal(bar, inc=1, device_id=(s, up), device_id_type=MESH)
    pl.semaphore_signal(bar, inc=1, device_id=(s, dn), device_id_type=MESH)
    pl.semaphore_wait(bar, 5)

    def head_cols(zhs, zs):
        return pl.ds(pl.multiple_of(((zhs * 4 + y) * 2 + zs) * HD, HD), HD)

    own = pltpu.make_async_copy(o_ref.at[z], a_ref.at[:, head_cols(zh, z)], loc_sem.at[0])
    own.start()
    outs = []
    for n, (zd, zhd) in enumerate(peers):
        cp = remote(
            o_ref.at[zd], a_ref.at[:, head_cols(zh, z)], send.at[n], recv.at[n],
            (seq_of(zd, x, c), zhd * 4 + y),
        )
        cp.start()
        outs.append(cp)
    own.wait()
    for n, (zd, zhd) in enumerate(peers):
        remote(
            o_ref.at[0], a_ref.at[:, head_cols(zhd, zd)], send.at[n], recv.at[n], (s, hd)
        ).wait_recv()

    def slab(zz, yy):
        return a_ref.at[:, pl.ds(pl.multiple_of((zz * 4 + yy) * 256, 256), 256)]

    def y_copy(n, zz, yy, dev):
        return remote(slab(zz, yy), slab(zz, yy), ysend.at[n], yrecv.at[yy * 2 + zz], (s, dev))

    y1 = lax.rem(y + 3, 4)
    y2 = lax.rem(y + 1, 4)
    y3 = lax.rem(y + 2, 4)
    sends = [y_copy(0, 0, y, up), y_copy(1, 1, y, dn), y_copy(2, 1, y, up), y_copy(3, 0, y, dn)]
    for cp in sends:
        cp.start()
    y_copy(0, 0, y1, up).wait_recv()
    f0 = y_copy(4, 0, y1, up)
    f0.start()
    y_copy(0, 1, y2, up).wait_recv()
    f1 = y_copy(5, 1, y2, dn)
    f1.start()
    for zz, yy in ((1, y1), (0, y2), (0, y3), (1, y3)):
        y_copy(0, zz, yy, up).wait_recv()
    for cp in outs + sends + [f0, f1]:
        cp.wait_send()


def gather(o):
    dma = pltpu.SemaphoreType.DMA
    vm = pl.BlockSpec(memory_space=pltpu.VMEM)
    return pl.pallas_call(
        gather_kernel,
        out_shape=jax.ShapeDtypeStruct((ROWS, 2048), jnp.bfloat16),
        in_specs=[vm],
        out_specs=vm,
        scratch_shapes=[dma((3,)), dma((3,)), dma((6,)), dma((8,)), dma((1,))],
        compiler_params=pltpu.CompilerParams(
            collective_id=1, has_side_effects=True, vmem_limit_bytes=32 << 20
        ),
        name="gather_heads",
    )(o)


def tables(block_index):
    z = lax.axis_index("seq") // 8
    w = block_index.reshape(-1)
    holder = w // 64
    local = w - holder * 64
    owners = jnp.arange(16, dtype=jnp.int32)
    n = jnp.arange(32, dtype=jnp.int32)
    same = holder[:, None] == holder[None, :]
    count = jnp.sum(same.astype(jnp.int32), axis=1)
    place = jnp.sum((same & (n[None, :] < n[:, None])).astype(jnp.int32), axis=1)
    is_hot = count == TOPB
    rank = jnp.sum((same & (local[None, :] < local[:, None])).astype(jnp.int32), axis=1)
    lanes = jnp.arange(128, dtype=jnp.int32)
    hit = (holder[:, None, None] == owners[None, :, None]) & (
        place[:, None, None] == lanes[None, None, :]
    ) & (lanes < 2)[None, None, :]
    req = jnp.sum(jnp.where(hit, local[:, None, None], 0), axis=0)
    code = jnp.where(is_hot, 64 + rank, (z * 16 + holder) * 2 + place)
    at_code = n[:, None] == lanes[None, :]
    at_hot = is_hot[:, None] & ((rank + 32)[:, None] == lanes[None, :])
    at_owner = (is_hot & (rank == 0))[:, None] & (lanes == 40)[None, :]
    info = jnp.sum(
        jnp.where(at_code, code[:, None], 0)
        + jnp.where(at_hot, local[:, None], 0)
        + jnp.where(at_owner, holder[:, None], 0),
        axis=0,
    )
    return (
        jnp.broadcast_to(req[:, None, :], (16, 8, 128)),
        jnp.broadcast_to(info[None, :], (8, 128)),
    )


def shards(q, k, v, mk, mv, block_index, w):
    req, info = tables(block_index)
    o, wc = attention(
        q, k, v, mk.reshape(-1, BLOCK, 2 * HD), mv.reshape(-1, BLOCK, 2 * HD), req, info, w
    )
    a = gather(o)
    return jnp.dot(a, wc, preferred_element_type=jnp.float32).astype(jnp.bfloat16)


def solution(mesh):
    return jax.shard_map(
        shards,
        mesh=mesh,
        in_specs=(
            P("seq", "head"), P("seq", "head"), P("seq", "head"), P("seq", "head"),
            P("seq", "head"), P("seq", None), P("head", None),
        ),
        out_specs=P("seq", "head"),
        check_vma=False,
    )
```

time: 584 us -> 166 us (0.28)
  the two profiles are of different devices: /device:TPU:0 before, /device:TPU:6 now
where the time goes in v1:
time: 166 us; the launch traced here: 165 us
  Pallas kernels  158 us (95%)
  matrix products  3.29 us (2%)
  local copies, waits for them, and re-layouts  3.03 us (2%)
    pallas_call x1, Pallas kernels, attention(): pl.pallas_call(attention_kernel, out_shape=(jax.ShapeDtypeStruct((2, ROWS...  103 us
    pallas_call x1, Pallas kernels, gather(): pl.pallas_call(gather_kernel, out_shape=jax.ShapeDtypeStruct((ROWS, 2048)...  54.9 us

profile of v1, /device:TPU:6, one launch (start us, length us, event | category | flops | bytes accessed | tf_op | source)
XLA Modules:
  0.0 165.5 jit_solution(16824242673654343245)
XLA Ops:
  0.0 0.8 reshape.224
  0.8 0.2 fusion
  1.0 0.1 add_reduce_fusion
  1.1 0.1 iota_compare_fusion.4
  1.2 0.6 broadcast_in_dim.77.info_ref
  1.8 0.1 iota_compare_fusion.2
  1.9 0.2 select_reduce_fusion
  2.1 0.6 broadcast_in_dim.42.req_ref
  2.7 103.5 %attention.1 = (bf16[2,1024,128]{2,1,0:T(8,128)(2,1)}, bf16[2048,512]{1,0:T(8,128)(2,1)}) custom-call(bf16[1024,256]{1,0:T(8,128)(2,1)} %q_hbm.1, bf16[1024,256]{1,0:T(8,128)(2,1)} %k_hbm.1, bf16[1024,256]{1,0:T(8,128)(2,1)} %v_hbm.1, bf16[64,64,256]{2,1,0:T(8,128)(2,1)} %bitcast.4, bf16[64,64,256]{2,1,0:T(8,128)(2,1)} %bitcast.5, ...), custom_call_target="tpu_custom_call" | custom-call | tf_op jit(solution)/shard_map/attention/pallas_call | solution.py:490
  106.2 0.0 copy-start
  106.2 1.0 copy-done
  107.2 0.0 copy-start.1
  107.2 54.9 %gather_heads.1 = bf16[1024,2048]{1,0:T(8,128)(2,1)S(1)} custom-call(bf16[2,1024,128]{2,1,0:T(8,128)(2,1)S(1)} %copy-done), custom_call_target="tpu_custom_call" | custom-call | tf_op jit(solution)/shard_map/gather_heads/pallas_call | solution.py:605
  162.2 0.0 copy-done.1
  162.2 3.3 %convolution_convert_fusion = bf16[1024,512]{1,0:T(8,128)(2,1)} fusion(bf16[1024,2048]{1,0:T(8,128)(2,1)S(1)} %gather_heads.1, bf16[2048,512]{1,0:T(8,128)(2,1)S(1)} %copy-done.1), kind=kOutput, calls=%fused_computation | convolution fusion | flops 2148007936 | bytes 7340032 | tf_op jit(solution)/shard_map/dot_general | solution.py:657
  (5 shorter events, 0.0 us)
Async XLA Ops:
  106.2 1.0 copy-start
  107.2 54.9 %copy-start.1 = (bf16[2048,512]{1,0:T(8,128)(2,1)S(1)}, bf16[2048,512]{1,0:T(8,128)(2,1)}, u32[]{:S(2)}) copy-start(bf16[2048,512]{1,0:T(8,128)(2,1)} %get-tuple-element.8) | copy-start | bytes 6291460

commit v2 on v1

--- a/solution.py
+++ b/solution.py
@@ -18,6 +18,8 @@
 SCALE = math.log2(math.e) / math.sqrt(HD)
 LOW = -1e30
 STEPS = 24
+MEM_NEAR = 12
+MEM_FAR = 13
 
 
 def where_am_i():
@@ -113,8 +115,7 @@
         remote(info_ref, infoin, swap_send.at[2], info_recv.at[0], (zp, hd)),
         remote(q_hbm.at[:, theirs], q.at[z], swap_send.at[3], q_recv.at[0], (zp, hd)),
     ]
-    for cp in swaps:
-        cp.start()
+    swaps[2].start()
 
     def req_copy(i):
         return remote(req_ref.at[i], reqin.at[s], req_send.at[i], req_recv.at[s], (i, hd))
@@ -126,6 +127,8 @@
         return 0
 
     lax.fori_loop(0, 16, send_req, 0)
+    swaps[0].start()
+    swaps[1].start()
 
     loc[0].wait()
     loc[1].wait()
@@ -161,6 +164,7 @@
 
     for cp in sends_of(0, z, s):
         cp.start()
+    swaps[3].start()
 
     def w_copy(i):
         cols = pl.ds(pl.multiple_of(i * 512, 512), 512)
@@ -355,11 +359,11 @@
             hm1[...] = jnp.where(keep, hown[...], hr0[...])
             hot_copies(1).start()
 
-        @pl.when(t == 6)
+        @pl.when((t == MEM_NEAR) | (t == MEM_FAR))
         def _():
             def send(i, _):
-                r = lax.rem(i // 2 + s + 1, 16)
-                e = lax.rem(i, 2)
+                r = lax.rem(i + s + 1, 16)
+                e = jnp.where(t == MEM_NEAR, z, 1 - z)
                 dst, at = mem_copy(r, e)
 
                 @pl.when(dst == s)
@@ -371,7 +375,7 @@
                     mem_remote(r, e).start()
                 return 0
 
-            lax.fori_loop(0, 32, send, 0)
+            lax.fori_loop(0, 16, send, 0)
 
         @pl.when(t == 7)
         def _():
@@ -542,10 +546,13 @@
     )(q, k, v, mk, mv, req, info, w)
 
 
-def gather_kernel(o_ref, a_ref, send, recv, ysend, yrecv, loc_sem):
+def gather_kernel(o_ref, a_ref, ybuf, send, recv, ysend, yrecv, loc_sem):
     s, hd, z, x, c, zh, y = where_am_i()
     up = zh * 4 + lax.rem(y + 1, 4)
     dn = zh * 4 + lax.rem(y + 3, 4)
+    y1 = lax.rem(y + 3, 4)
+    y2 = lax.rem(y + 1, 4)
+    y3 = lax.rem(y + 2, 4)
     peers = [(1 - z, zh), (1 - z, 1 - zh), (z, 1 - zh)]
     bar = pltpu.get_barrier_semaphore()
     for zd, zhd in peers:
@@ -556,47 +563,104 @@
     pl.semaphore_signal(bar, inc=1, device_id=(s, dn), device_id_type=MESH)
     pl.semaphore_wait(bar, 5)
 
-    def head_cols(zhs, zs):
-        return pl.ds(pl.multiple_of(((zhs * 4 + y) * 2 + zs) * HD, HD), HD)
-
-    own = pltpu.make_async_copy(o_ref.at[z], a_ref.at[:, head_cols(zh, z)], loc_sem.at[0])
-    own.start()
-    outs = []
-    for n, (zd, zhd) in enumerate(peers):
-        cp = remote(
-            o_ref.at[zd], a_ref.at[:, head_cols(zh, z)], send.at[n], recv.at[n],
+    def head_cols(zhs, ys, zs):
+        return pl.ds(pl.multiple_of(((zhs * 4 + ys) * 2 + zs) * HD, HD), HD)
+
+    def z_send(src, ys, p, n):
+        zd, zhd = peers[p]
+        return remote(
+            src(zd), a_ref.at[:, head_cols(zh, ys, z)], send.at[n * 3 + p], recv.at[n * 3 + p],
             (seq_of(zd, x, c), zhd * 4 + y),
         )
-        cp.start()
-        outs.append(cp)
-    own.wait()
-    for n, (zd, zhd) in enumerate(peers):
+
+    def z_wait(ys, p, n):
+        zd, zhd = peers[p]
         remote(
-            o_ref.at[0], a_ref.at[:, head_cols(zhd, zd)], send.at[n], recv.at[n], (s, hd)
+            o_ref.at[0], a_ref.at[:, head_cols(zhd, ys, zd)], send.at[n * 3 + p],
+            recv.at[n * 3 + p], (s, hd),
         ).wait_recv()
 
-    def slab(zz, yy):
-        return a_ref.at[:, pl.ds(pl.multiple_of((zz * 4 + yy) * 256, 256), 256)]
-
-    def y_copy(n, zz, yy, dev):
-        return remote(slab(zz, yy), slab(zz, yy), ysend.at[n], yrecv.at[yy * 2 + zz], (s, dev))
-
-    y1 = lax.rem(y + 3, 4)
-    y2 = lax.rem(y + 1, 4)
-    y3 = lax.rem(y + 2, 4)
-    sends = [y_copy(0, 0, y, up), y_copy(1, 1, y, dn), y_copy(2, 1, y, up), y_copy(3, 0, y, dn)]
-    for cp in sends:
-        cp.start()
-    y_copy(0, 0, y1, up).wait_recv()
-    f0 = y_copy(4, 0, y1, up)
-    f0.start()
-    y_copy(0, 1, y2, up).wait_recv()
-    f1 = y_copy(5, 1, y2, dn)
-    f1.start()
-    for zz, yy in ((1, y1), (0, y2), (0, y3), (1, y3)):
-        y_copy(0, zz, yy, up).wait_recv()
-    for cp in outs + sends + [f0, f1]:
-        cp.wait_send()
+    own = pltpu.make_async_copy(o_ref.at[z], a_ref.at[:, head_cols(zh, y, z)], loc_sem.at[0])
+    own.start()
+    outs = [z_send(lambda zd: o_ref.at[zd], y, p, 0) for p in range(3)]
+
+    @pl.when(c == 0)
+    def _():
+        for cp in outs:
+            cp.start()
+        own.wait()
+        for p in range(3):
+            z_wait(y, p, 0)
+
+        def slab(zz, yy):
+            return a_ref.at[:, pl.ds(pl.multiple_of((zz * 4 + yy) * 256, 256), 256)]
+
+        def y_copy(n, zz, yy, dev):
+            return remote(slab(zz, yy), slab(zz, yy), ysend.at[n], yrecv.at[yy * 2 + zz], (s, dev))
+
+        sends = [y_copy(0, 0, y, up), y_copy(1, 1, y, dn), y_copy(2, 1, y, up), y_copy(3, 0, y, dn)]
+        for cp in sends:
+            cp.start()
+        y_copy(0, 0, y1, up).wait_recv()
+        f0 = y_copy(4, 0, y1, up)
+        f0.start()
+        y_copy(0, 1, y2, up).wait_recv()
+        f1 = y_copy(5, 1, y2, dn)
+        f1.start()
+        for zz, yy in ((1, y1), (0, y2), (0, y3), (1, y3)):
+            y_copy(0, zz, yy, up).wait_recv()
+        for cp in outs + sends + [f0, f1]:
+            cp.wait_send()
+
+    @pl.when(c == 1)
+    def _():
+        def y_copy(n, h, yy, dev, first=False):
+            src = o_ref.at[h] if first else ybuf.at[yy, h]
+            return remote(src, ybuf.at[yy, h], ysend.at[n], yrecv.at[yy * 2 + h], (s, dev))
+
+        sends = [
+            y_copy(0, 0, y, up, True), y_copy(1, 1, y, dn, True),
+            y_copy(2, 1, y, up, True), y_copy(3, 0, y, dn, True),
+        ]
+        for cp in sends:
+            cp.start()
+        for cp in outs:
+            cp.start()
+        y_copy(0, 0, y1, up).wait_recv()
+        f0 = y_copy(4, 0, y1, up)
+        f0.start()
+        y_copy(0, 1, y2, up).wait_recv()
+        f1 = y_copy(5, 1, y2, dn)
+        f1.start()
+        locs = []
+        more = []
+
+        def spread(yy, n):
+            cps = [z_send(lambda zd: ybuf.at[yy, zd], yy, p, n) for p in range(3)]
+            for cp in cps:
+                cp.start()
+            lc = pltpu.make_async_copy(
+                ybuf.at[yy, z], a_ref.at[:, head_cols(zh, yy, z)], loc_sem.at[n]
+            )
+            lc.start()
+            more.extend(cps)
+            locs.append(lc)
+
+        y_copy(0, 1, y1, up).wait_recv()
+        spread(y1, 1)
+        y_copy(0, 0, y2, up).wait_recv()
+        spread(y2, 2)
+        y_copy(0, 0, y3, up).wait_recv()
+        y_copy(0, 1, y3, up).wait_recv()
+        spread(y3, 3)
+        own.wait()
+        for lc in locs:
+            lc.wait()
+        for n, yy in enumerate((y, y1, y2, y3)):
+            for p in range(3):
+                z_wait(yy, p, n)
+        for cp in outs + sends + more + [f0, f1]:
+            cp.wait_send()
 
 
 def gather(o):
@@ -607,7 +671,10 @@
         out_shape=jax.ShapeDtypeStruct((ROWS, 2048), jnp.bfloat16),
         in_specs=[vm],
         out_specs=vm,
-        scratch_shapes=[dma((3,)), dma((3,)), dma((6,)), dma((8,)), dma((1,))],
+        scratch_shapes=[
+            pltpu.VMEM((4, 2, ROWS, HD), jnp.bfloat16),
+            dma((12,)), dma((12,)), dma((6,)), dma((8,)), dma((4,)),
+        ],
         compiler_params=pltpu.CompilerParams(
             collective_id=1, has_side_effects=True, vmem_limit_bytes=32 << 20
         ),

time: 166 us -> 132 us (0.80)
  the two profiles are of different devices: /device:TPU:6 before, /device:TPU:0 now
where the time goes in v2:
time: 132 us
  Pallas kernels  125 us (95%)
  matrix products  3.31 us (3%)
  local copies, waits for them, and re-layouts  3.03 us (2%)
    pallas_call x1, Pallas kernels, attention(): pl.pallas_call(attention_kernel, out_shape=(jax.ShapeDtypeStruct((2, ROWS...  86.3 us
    pallas_call x1, Pallas kernels, gather(): pl.pallas_call(gather_kernel, out_shape=jax.ShapeDtypeStruct((ROWS, 2048)...  38.3 us
    dot_general x1, matrix products, shards(): jnp.dot(a, wc, preferred_element_type=jnp.float32).astype(jnp.bfloat16)  3.31 us

profile of v2, /device:TPU:0, one launch (start us, length us, event | category | flops | bytes accessed | tf_op | source)
XLA Modules:
  0.0 131.7 jit_solution(11312992192515168686)
XLA Ops:
  0.0 0.8 reshape.224
  0.8 0.2 fusion
  1.0 0.1 add_reduce_fusion
  1.1 0.1 iota_compare_fusion.4
  1.2 0.6 broadcast_in_dim.77.info_ref
  1.8 0.1 iota_compare_fusion.2
  1.9 0.2 select_reduce_fusion
  2.1 0.6 broadcast_in_dim.42.req_ref
  2.7 86.3 %attention.1 = (bf16[2,1024,128]{2,1,0:T(8,128)(2,1)}, bf16[2048,512]{1,0:T(8,128)(2,1)}) custom-call(bf16[1024,256]{1,0:T(8,128)(2,1)} %q_hbm.1, bf16[1024,256]{1,0:T(8,128)(2,1)} %k_hbm.1, bf16[1024,256]{1,0:T(8,128)(2,1)} %v_hbm.1, bf16[64,64,256]{2,1,0:T(8,128)(2,1)} %bitcast.4, bf16[64,64,256]{2,1,0:T(8,128)(2,1)} %bitcast.5, ...), custom_call_target="tpu_custom_call" | custom-call | tf_op jit(solution)/shard_map/attention/pallas_call | solution.py:494
  89.0 0.0 copy-start
  89.0 1.0 copy-done
  90.0 0.0 copy-start.1
  90.0 38.3 %gather_heads.1 = bf16[1024,2048]{1,0:T(8,128)(2,1)S(1)} custom-call(bf16[2,1024,128]{2,1,0:T(8,128)(2,1)S(1)} %copy-done), custom_call_target="tpu_custom_call" | custom-call | tf_op jit(solution)/shard_map/gather_heads/pallas_call | solution.py:669
  128.4 0.0 copy-done.1
  128.4 3.3 %convolution_convert_fusion = bf16[1024,512]{1,0:T(8,128)(2,1)} fusion(bf16[1024,2048]{1,0:T(8,128)(2,1)S(1)} %gather_heads.1, bf16[2048,512]{1,0:T(8,128)(2,1)S(1)} %copy-done.1), kind=kOutput, calls=%fused_computation | convolution fusion | flops 2148007936 | bytes 7340032 | tf_op jit(solution)/shard_map/dot_general | solution.py:724
  (5 shorter events, 0.0 us)
Async XLA Ops:
  89.0 1.0 copy-start
  90.0 38.3 %copy-start.1 = (bf16[2048,512]{1,0:T(8,128)(2,1)S(1)}, bf16[2048,512]{1,0:T(8,128)(2,1)}, u32[]{:S(2)}) copy-start(bf16[2048,512]{1,0:T(8,128)(2,1)} %get-tuple-element.8) | copy-start | bytes 6291460

commit v3 on v2

--- a/solution.py
+++ b/solution.py
@@ -18,8 +18,9 @@
 SCALE = math.log2(math.e) / math.sqrt(HD)
 LOW = -1e30
 STEPS = 24
-MEM_NEAR = 12
-MEM_FAR = 13
+GATHER_AT = 1
+MEM_NEAR = 9
+MEM_FAR = 12
 
 
 def where_am_i():
@@ -51,21 +52,19 @@
 
 DXS = (0, 0, 3, 1, 3, 1, 2, 2)
 SIBS = (0, 1, 0, 0, 1, 1, 0, 1)
-SERVICE_A = {1: 1, 2: 2, 4: 4, 5: 5, 6: 8, 7: 7, 10: 9, 12: 10, 16: 12, 18: 13, 20: 14, 22: 15}
-SERVICE_B = {2: 3, 6: 6, 12: 11}
+SERVICE_A = {1: 1, 2: 2, 3: 8, 4: 4, 5: 5, 6: 6, 7: 7, 10: 9, 12: 10, 16: 12, 18: 13, 20: 14, 22: 15}
+SERVICE_B = {2: 3, 12: 11}
 
 
 def attention_kernel(
     q_hbm, k_hbm, v_hbm, mk_hbm, mv_hbm, req_ref, info_ref, w_hbm,
     o_ref, wc_hbm,
-    q, kv, m_s, l_s, acc, mk, mv, stage, mem, kc, vc,
-    hsend, hown, hr0, hm1, hr1, hm2, hr2, hm3, hr3,
+    q, kv, m_s, l_s, acc, mk, mv, stage, mem, hot, kc, vc,
     reqin, infoin, reqs, infos,
     loc_sem, kv_recv, ring_send, swap_send, q_recv, info_recv,
     req_send, req_recv, mem_send, mem_recv, hot_send, hot_recv, w_send, w_recv,
 ):
     s, hd, z, x, c, zh, y = where_am_i()
-    me = s
     zp = seq_of(1 - z, x, c)
     sib = seq_of(z, x, 1 - c)
     xr = seq_of(z, lax.rem(x + 1, 4), c)
@@ -130,40 +129,35 @@
     swaps[0].start()
     swaps[1].start()
 
-    loc[0].wait()
-    loc[1].wait()
-
     def ring_copy(half, n, g, k, dev):
         return remote(
             kv.at[g, k], kv.at[g, k], ring_send.at[half * 14 + n], kv_recv.at[g * 2 + k], (dev, hd)
         )
 
-    def sends_of(kind, half, g):
+    def sends_of(kind, half, g, k):
         if kind == 0:
+            n = 3 * k
             return [
-                ring_copy(half, 0, g, 0, xr), ring_copy(half, 1, g, 0, xl),
-                ring_copy(half, 2, g, 1, xr), ring_copy(half, 3, g, 1, xl),
-                ring_copy(half, 4, g, 0, sib), ring_copy(half, 5, g, 1, sib),
+                ring_copy(half, n, g, k, xr), ring_copy(half, n + 1, g, k, xl),
+                ring_copy(half, n + 2, g, k, sib),
             ]
         if kind == 2:
-            return [
-                ring_copy(half, 6, g, 0, xr),
-                ring_copy(half, 7, g, 0, sib), ring_copy(half, 8, g, 1, sib),
-            ]
+            on = [ring_copy(half, 6, g, 0, xr)] if k == 0 else []
+            return on + [ring_copy(half, 7 + k, g, k, sib)]
         if kind == 3:
-            return [
-                ring_copy(half, 9, g, 1, xl),
-                ring_copy(half, 10, g, 0, sib), ring_copy(half, 11, g, 1, sib),
-            ]
-        return [ring_copy(half, 12, g, 0, sib), ring_copy(half, 13, g, 1, sib)]
+            on = [ring_copy(half, 9, g, 1, xl)] if k == 1 else []
+            return on + [ring_copy(half, 10 + k, g, k, sib)]
+        return [ring_copy(half, 12 + k, g, k, sib)]
 
     def block_of(half, i):
         dx = pick(i, dict(enumerate(DXS)), 0)
         sb = pick(i, dict(enumerate(SIBS)), 0)
         return seq_of(half, lax.rem(x + dx, 4), jnp.where(sb == 1, 1 - c, c))
 
-    for cp in sends_of(0, z, s):
-        cp.start()
+    for k in range(2):
+        loc[k].wait()
+        for cp in sends_of(0, z, s, k):
+            cp.start()
     swaps[3].start()
 
     def w_copy(i):
@@ -191,9 +185,8 @@
     l_s[...] = jnp.zeros_like(l_s)
     acc[...] = jnp.zeros_like(acc)
 
-    def wait_block(g):
-        for k in range(2):
-            remote(kv.at[g, k], kv.at[g, k], ring_send.at[0], kv_recv.at[g * 2 + k], (sib, hd)).wait_recv()
+    def wait_part(g, k):
+        remote(kv.at[g, k], kv.at[g, k], ring_send.at[0], kv_recv.at[g * 2 + k], (sib, hd)).wait_recv()
 
     def service(code):
         @pl.when(code >= 0)
@@ -201,12 +194,13 @@
             half = jnp.where(code >= 8, 1 - z, z)
             i = lax.rem(code, 8)
             g = block_of(half, i)
-            wait_block(g)
-            for kind in (0, 2, 3, 6):
-                @pl.when(i == kind)
-                def _(kind=kind):
-                    for cp in sends_of(kind, half, g):
-                        cp.start()
+            for k in range(2):
+                wait_part(g, k)
+                for kind in (0, 2, 3, 6):
+                    @pl.when(i == kind)
+                    def _(kind=kind):
+                        for cp in sends_of(kind, half, g, k):
+                            cp.start()
 
     def pipelined(n, scores, finish):
         state = scores(0)
@@ -277,25 +271,9 @@
             stage.at[r, e], pair(at), mem_send.at[r * 2 + e], mem_recv.at[at], (dst, hd)
         )
 
-    def hot_copy(n, src, dst, dev):
-        return remote(src, dst, hot_send.at[n], hot_recv.at[n], (dev, hd))
-
-    hx1 = seq_of(z, jnp.where(x % 2 == 0, x + 1, x - 1), c)
-    hx2 = seq_of(z, 3 - x, c)
-
     def hot_copies(n):
-        if n == 0:
-            return hot_copy(0, hsend, hr0, sib)
-        if n == 1:
-            return hot_copy(1, hm1.at[1 - z], hr1, zp)
-        if n == 2:
-            return hot_copy(2, hm2, hr2, hx1)
-        if n == 3:
-            return hot_copy(3, hm3, hr3, hx2)
-        return hot_copy(4, mem.at[pl.ds(64, 8), c], mem.at[pl.ds(64, 8), c], sib)
-
-    def hot_owner():
-        return infos[z, 0, 40]
+        at = pl.ds(4 * n + 2 * c, 2)
+        return remote(hot.at[at], hot.at[at], hot_send.at[n], hot_recv.at[n], (sib, hd))
 
     def step(t, _):
         @pl.when(t == 8)
@@ -305,7 +283,7 @@
         service(pick(t, SERVICE_A, -1))
         service(pick(t, SERVICE_B, -1))
 
-        @pl.when(t == 1)
+        @pl.when(t == GATHER_AT)
         def _():
             def wait_req(i, _):
                 @pl.when(i != s)
@@ -326,19 +304,6 @@
             a.wait()
             b.wait()
 
-            def hot_rows(j, _):
-                b = infos[z, 0, 32 + j]
-                kr = mk[b]
-                vr = mv[b]
-                for e in range(2):
-                    cols = slice(e * HD, (e + 1) * HD)
-                    hown[e, j] = jnp.where(c == 0, kr[:, cols], vr[:, cols])
-                    hsend[e, j] = jnp.where(c == 0, vr[:, cols], kr[:, cols])
-                return 0
-
-            lax.fori_loop(0, 8, hot_rows, 0)
-            hot_copies(0).start()
-
             def gather(r, _):
                 for b2 in range(2):
                     b = reqs[r, 0, b2]
@@ -352,13 +317,6 @@
 
             lax.fori_loop(0, 16, gather, 0)
 
-        @pl.when(t == 4)
-        def _():
-            hot_copies(0).wait_recv()
-            keep = hot_owner() == me
-            hm1[...] = jnp.where(keep, hown[...], hr0[...])
-            hot_copies(1).start()
-
         @pl.when((t == MEM_NEAR) | (t == MEM_FAR))
         def _():
             def send(i, _):
@@ -376,28 +334,6 @@
                 return 0
 
             lax.fori_loop(0, 16, send, 0)
-
-        @pl.when(t == 7)
-        def _():
-            hot_copies(1).wait_recv()
-            keep = (hot_owner() // 8) == z
-            hm2[...] = jnp.where(keep, hm1[z], hr1[...])
-            hot_copies(2).start()
-
-        @pl.when(t == 11)
-        def _():
-            hot_copies(2).wait_recv()
-            keep = ((hot_owner() // 2) % 4) == x
-            hm3[...] = jnp.where(keep, hm2[...], hr2[...])
-            hot_copies(3).start()
-
-        @pl.when(t == 14)
-        def _():
-            hot_copies(3).wait_recv()
-            keep = ((hot_owner() // 4) % 2) == (x // 2)
-            for j in range(8):
-                mem[64 + j, c] = jnp.where(keep, hm3[j], hr3[j])
-            hot_copies(4).start()
 
         native = t < 8
         u = t - 8
@@ -411,21 +347,30 @@
     lax.fori_loop(0, STEPS, step, 0)
 
     def wait_mem(i, _):
-        o = lax.rem(i, 16)
-
-        @pl.when(o != s)
-        def _():
-            remote(stage.at[0, 0], pair(i), mem_send.at[0], mem_recv.at[i], (sib, hd)).wait_recv()
-
-        @pl.when(o == s)
+        own = lax.rem(i, 16) == s
+
+        @pl.when(jnp.logical_not(own))
+        def _():
+            remote(
+                stage.at[0, 0], pair(i), mem_send.at[0], mem_recv.at[i], (sib, hd)
+            ).wait_recv()
+
+        @pl.when(own)
         def _():
             pltpu.make_async_copy(stage.at[0, 0], pair(i), mem_recv.at[i]).wait()
         return 0
 
     lax.fori_loop(0, 32, wait_mem, 0)
-    remote(
-        mem.at[pl.ds(64, 8), 0], mem.at[pl.ds(64, 8), 1 - c], hot_send.at[4], hot_recv.at[4], (sib, hd)
-    ).wait_recv()
+    ho = infos[z, 0, 40]
+    for n in range(2):
+        for b2 in range(2):
+            hot[4 * n + 2 * c + b2] = mem[(n * 16 + ho) * 2 + b2]
+        hot_copies(n).start()
+    for n in range(2):
+        at = pl.ds(4 * n + 2 * (1 - c), 2)
+        remote(hot.at[at], hot.at[at], hot_send.at[n], hot_recv.at[n], (sib, hd)).wait_recv()
+    for j in range(8):
+        mem[64 + j] = hot[j]
 
     def mem_group(i, _):
         qh = i // 4
@@ -448,9 +393,10 @@
         cp.wait_send()
     for half in (0, 1):
         for kind in (0, 2, 3, 6):
-            for cp in sends_of(kind, half, s):
-                cp.wait_send()
-    for n in range(5):
+            for k in range(2):
+                for cp in sends_of(kind, half, s, k):
+                    cp.wait_send()
+    for n in range(2):
         hot_copies(n).wait_send()
 
     def drain_req(i, _):
@@ -489,7 +435,6 @@
     any_ = pl.BlockSpec(memory_space=pl.ANY)
     vm = pl.BlockSpec(memory_space=pltpu.VMEM)
     b16 = jnp.bfloat16
-    hot = (8, BLOCK, HD)
     dma = pltpu.SemaphoreType.DMA
     return pl.pallas_call(
         attention_kernel,
@@ -509,17 +454,9 @@
             pltpu.VMEM((64, BLOCK, 2 * HD), b16),
             pltpu.VMEM((16, 2, 2, 2, BLOCK, HD), b16),
             pltpu.VMEM((72, 2, BLOCK, HD), b16),
+            pltpu.VMEM((8, 2, BLOCK, HD), b16),
             pltpu.VMEM((TOPB * BLOCK, HD), b16),
             pltpu.VMEM((TOPB * BLOCK, HD), b16),
-            pltpu.VMEM((2,) + hot, b16),
-            pltpu.VMEM((2,) + hot, b16),
-            pltpu.VMEM((2,) + hot, b16),
-            pltpu.VMEM((2,) + hot, b16),
-            pltpu.VMEM(hot, b16),
-            pltpu.VMEM(hot, b16),
-            pltpu.VMEM(hot, b16),
-            pltpu.VMEM(hot, b16),
-            pltpu.VMEM(hot, b16),
             pltpu.VMEM((16, 8, 128), jnp.int32),
             pltpu.VMEM((8, 128), jnp.int32),
             pltpu.SMEM((16, 8, 128), jnp.int32),
@@ -534,8 +471,8 @@
             dma((16,)),
             dma((32,)),
             dma((32,)),
-            dma((5,)),
-            dma((5,)),
+            dma((2,)),
+            dma((2,)),
             dma((8,)),
             dma((8,)),
         ],
@@ -695,8 +632,10 @@
     is_hot = count == TOPB
     rank = jnp.sum((same & (local[None, :] < local[:, None])).astype(jnp.int32), axis=1)
     lanes = jnp.arange(128, dtype=jnp.int32)
+    mine = z * 2 + lax.axis_index("seq") % 2
+    slot = jnp.where(is_hot, rank - 2 * mine, place)
     hit = (holder[:, None, None] == owners[None, :, None]) & (
-        place[:, None, None] == lanes[None, None, :]
+        slot[:, None, None] == lanes[None, None, :]
     ) & (lanes < 2)[None, None, :]
     req = jnp.sum(jnp.where(hit, local[:, None, None], 0), axis=0)
     code = jnp.where(is_hot, 64 + rank, (z * 16 + holder) * 2 + place)

time: 132 us -> 127 us (0.962)
  Pallas kernels: 125 us -> 120 us
    pallas_call x1, Pallas kernels: 86.3 us -> 82.1 us  [attention(): pl.pallas_call(attention_kernel, out_shape=(jax.ShapeDtypeStruct((2, ROWS...]
where the time goes in v3:
time: 127 us
  Pallas kernels  120 us (94%)
  matrix products  3.29 us (3%)
  local copies, waits for them, and re-layouts  3.03 us (2%)
    pallas_call x1, Pallas kernels, attention(): pl.pallas_call(attention_kernel, out_shape=(jax.ShapeDtypeStruct((2, ROWS...  82.1 us
    pallas_call x1, Pallas kernels, gather(): pl.pallas_call(gather_kernel, out_shape=jax.ShapeDtypeStruct((ROWS, 2048)...  37.5 us
    dot_general x1, matrix products, shards(): jnp.dot(a, wc, preferred_element_type=jnp.float32).astype(jnp.bfloat16)  3.29 us

profile of v3, /device:TPU:0, one launch (start us, length us, event | category | flops | bytes accessed | tf_op | source)
XLA Modules:
  0.0 126.7 jit_solution(6850649491997933270)
XLA Ops:
  0.0 0.8 reshape.234
  0.8 0.2 fusion
  1.0 0.1 add_reduce_fusion
  1.1 0.1 iota_compare_fusion.4
  1.2 0.6 broadcast_in_dim.77.info_ref
  1.8 0.1 iota_compare_fusion.2
  1.9 0.2 select_reduce_fusion
  2.1 0.6 broadcast_in_dim.42.req_ref
  2.7 82.1 %attention.1 = (bf16[2,1024,128]{2,1,0:T(8,128)(2,1)}, bf16[2048,512]{1,0:T(8,128)(2,1)}) custom-call(bf16[1024,256]{1,0:T(8,128)(2,1)} %q_hbm.1, bf16[1024,256]{1,0:T(8,128)(2,1)} %k_hbm.1, bf16[1024,256]{1,0:T(8,128)(2,1)} %v_hbm.1, bf16[64,64,256]{2,1,0:T(8,128)(2,1)} %bitcast.4, bf16[64,64,256]{2,1,0:T(8,128)(2,1)} %bitcast.5, ...), custom_call_target="tpu_custom_call" | custom-call | tf_op jit(solution)/shard_map/attention/pallas_call | solution.py:439
  84.8 0.0 copy-start
  84.8 1.0 copy-done
  85.8 0.0 copy-start.1
  85.8 37.5 %gather_heads.1 = bf16[1024,2048]{1,0:T(8,128)(2,1)S(1)} custom-call(bf16[2,1024,128]{2,1,0:T(8,128)(2,1)S(1)} %copy-done), custom_call_target="tpu_custom_call" | custom-call | tf_op jit(solution)/shard_map/gather_heads/pallas_call | solution.py:606
  123.4 0.0 copy-done.1
  123.4 3.3 %convolution_convert_fusion = bf16[1024,512]{1,0:T(8,128)(2,1)} fusion(bf16[1024,2048]{1,0:T(8,128)(2,1)S(1)} %gather_heads.1, bf16[2048,512]{1,0:T(8,128)(2,1)S(1)} %copy-done.1), kind=kOutput, calls=%fused_computation | convolution fusion | flops 2148007936 | bytes 7340032 | tf_op jit(solution)/shard_map/dot_general | solution.py:663
  (5 shorter events, 0.0 us)
Async XLA Ops:
  84.8 1.0 copy-start
  85.8 37.5 %copy-start.1 = (bf16[2048,512]{1,0:T(8,128)(2,1)S(1)}, bf16[2048,512]{1,0:T(8,128)(2,1)}, u32[]{:S(2)}) copy-start(bf16[2048,512]{1,0:T(8,128)(2,1)} %get-tuple-element.8) | copy-start | bytes 6291460

commit v4 on v3

--- a/solution.py
+++ b/solution.py
@@ -58,13 +58,19 @@
 
 def attention_kernel(
     q_hbm, k_hbm, v_hbm, mk_hbm, mv_hbm, req_ref, info_ref, w_hbm,
-    o_ref, wc_hbm,
-    q, kv, m_s, l_s, acc, mk, mv, stage, mem, hot, kc, vc,
+    out_ref,
+    q, kv, m_s, l_s, acc, mk, mv, stage, mem, hot, kc, vc, o, ybuf, a_ref, wc, total,
     reqin, infoin, reqs, infos,
     loc_sem, kv_recv, ring_send, swap_send, q_recv, info_recv,
     req_send, req_recv, mem_send, mem_recv, hot_send, hot_recv, w_send, w_recv,
+    zs, zr, ys, yr, as_,
 ):
     s, hd, z, x, c, zh, y = where_am_i()
+    up = zh * 4 + lax.rem(y + 1, 4)
+    dn = zh * 4 + lax.rem(y + 3, 4)
+    yy1 = lax.rem(y + 3, 4)
+    yy2 = lax.rem(y + 1, 4)
+    yy3 = lax.rem(y + 2, 4)
     zp = seq_of(1 - z, x, c)
     sib = seq_of(z, x, 1 - c)
     xr = seq_of(z, lax.rem(x + 1, 4), c)
@@ -106,7 +112,8 @@
         return 0
 
     lax.fori_loop(0, 8, greet_w, 0)
-    pl.semaphore_wait(bar, 22)
+    pl.semaphore_signal(bar, inc=1, device_id=(s, (1 - zh) * 4 + y), device_id_type=MESH)
+    pl.semaphore_wait(bar, 23)
 
     swaps = [
         remote(k_hbm.at[:, theirs], kv.at[s, 0], swap_send.at[0], kv_recv.at[s * 2], (zp, hd)),
@@ -164,7 +171,7 @@
         cols = pl.ds(pl.multiple_of(i * 512, 512), 512)
         rows = pl.ds(pl.multiple_of(hd * 256, 256), 256)
         return remote(
-            w_hbm.at[:, cols], wc_hbm.at[rows, :], w_send.at[i], w_recv.at[hd], w_target(i)
+            w_hbm.at[:, cols], wc.at[rows, :], w_send.at[i], w_recv.at[hd], w_target(i)
         )
 
     def send_w(i, _):
@@ -176,7 +183,7 @@
     lax.fori_loop(0, 8, send_w, 0)
     w_local = pltpu.make_async_copy(
         w_hbm.at[:, pl.ds(pl.multiple_of(hd * 512, 512), 512)],
-        wc_hbm.at[pl.ds(pl.multiple_of(hd * 256, 256), 256), :],
+        wc.at[pl.ds(pl.multiple_of(hd * 256, 256), 256), :],
         loc_sem.at[7],
     )
     w_local.start()
@@ -275,6 +282,157 @@
         at = pl.ds(4 * n + 2 * c, 2)
         return remote(hot.at[at], hot.at[at], hot_send.at[n], hot_recv.at[n], (sib, hd))
 
+    def head_cols(zhs, yy, zz):
+        return pl.ds(pl.multiple_of(((zhs * 4 + yy) * 2 + zz) * HD, HD), HD)
+
+    def z_send(h, n, yy, src, zhd):
+        at = (h * 4 + n) * 4 + z * 2 + zh
+        return remote(
+            src, a_ref.at[:, head_cols(zh, yy, z)],
+            zs.at[(h * 4 + n) * 2 + jnp.where(zhd == zh, 0, 1)], zr.at[at],
+            (seq_of(h, x, c), zhd * 4 + y),
+        )
+
+    def z_local(h, n, yy, src):
+        return pltpu.make_async_copy(src, a_ref.at[:, head_cols(zh, yy, z)], as_.at[h * 4 + n])
+
+    def z_start(h, n, yy, src):
+        z_send(h, n, yy, src, 1 - zh).start()
+
+        @pl.when(z == h)
+        def _():
+            z_local(h, n, yy, src).start()
+
+        @pl.when(z != h)
+        def _():
+            z_send(h, n, yy, src, zh).start()
+
+    def z_arrived(h, n, yy):
+        z_local(h, n, yy, o.at[0]).wait()
+        for zz, zhs in ((h, 1 - zh), (1 - h, zh), (1 - h, 1 - zh)):
+            at = (h * 4 + n) * 4 + zz * 2 + zhs
+            remote(
+                o.at[0], a_ref.at[:, head_cols(zhs, yy, zz)], zs.at[0], zr.at[at], (sib, hd)
+            ).wait_recv()
+
+    def z_left(h, n, yy, src):
+        z_send(h, n, yy, src, 1 - zh).wait_send()
+
+        @pl.when(z != h)
+        def _():
+            z_send(h, n, yy, src, zh).wait_send()
+
+    def slab(zz, yy):
+        return a_ref.at[:, pl.ds(pl.multiple_of((zz * 4 + yy) * 256, 256), 256)]
+
+    def y_slab(h, n, zz, yy, dev):
+        return remote(
+            slab(zz, yy), slab(zz, yy), ys.at[h * 6 + n], yr.at[h * 8 + yy * 2 + zz], (s, dev)
+        )
+
+    def y_part(h, n, part, yy, dev, first=False):
+        rows = pl.ds(part * 512, 512)
+        src = o.at[h, rows] if first else ybuf.at[yy, h, rows]
+        return remote(
+            src, ybuf.at[yy, h, rows], ys.at[h * 6 + n], yr.at[h * 8 + yy * 2 + part], (s, dev)
+        )
+
+    def y_own(h, f, **kw):
+        return [
+            f(h, 0, 0, y, up, **kw), f(h, 1, 1, y, dn, **kw),
+            f(h, 2, 1, y, up, **kw), f(h, 3, 0, y, dn, **kw),
+        ]
+
+    def turn(h, f):
+        f(h, 0, 0, yy1, up).wait_recv()
+        f(h, 4, 0, yy1, up).start()
+        f(h, 0, 1, yy2, up).wait_recv()
+        f(h, 5, 1, yy2, dn).start()
+
+    def heads_start(h):
+        @pl.when(c == 1)
+        def _():
+            for cp in y_own(h, y_part, first=True):
+                cp.start()
+
+        @pl.when(c == 0)
+        def _():
+            z_start(h, 0, y, o.at[h])
+
+    def heads_mid(h):
+        @pl.when((c == 0) & (z == h))
+        def _():
+            z_arrived(h, 0, y)
+            for cp in y_own(h, y_slab):
+                cp.start()
+
+        @pl.when(c == 1)
+        def _():
+            turn(h, y_part)
+            z_start(h, 0, y, o.at[h])
+
+    def heads_near(h):
+        @pl.when(c == 1)
+        def _():
+            y_part(h, 0, 1, yy1, up).wait_recv()
+            z_start(h, 1, yy1, ybuf.at[yy1, h])
+            y_part(h, 0, 0, yy2, up).wait_recv()
+            z_start(h, 2, yy2, ybuf.at[yy2, h])
+
+    def heads_fwd(h):
+        @pl.when((c == 0) & (z == h))
+        def _():
+            turn(h, y_slab)
+
+        @pl.when(c == 1)
+        def _():
+            y_part(h, 0, 0, yy3, up).wait_recv()
+            y_part(h, 0, 1, yy3, up).wait_recv()
+            z_start(h, 3, yy3, ybuf.at[yy3, h])
+
+    def project(zz, yy):
+        at = pl.ds(pl.multiple_of((zz * 4 + yy) * 256, 256), 256)
+
+        def part(j, _):
+            rows = pl.ds(pl.multiple_of(j * CHUNK, CHUNK), CHUNK)
+            total[rows, :] += jnp.dot(
+                a_ref[rows, at], wc[at, :], preferred_element_type=jnp.float32
+            )
+            return 0
+
+        lax.fori_loop(0, ROWS // CHUNK, part, 0)
+
+    def heads_end(h):
+        @pl.when((c == 0) & (z == h))
+        def _():
+            project(0, y)
+            project(1, y)
+            project(0, yy1)
+            project(1, yy2)
+            for zz, yy in ((1, yy1), (0, yy2), (0, yy3), (1, yy3)):
+                y_slab(h, 0, zz, yy, up).wait_recv()
+                project(zz, yy)
+            for cp in y_own(h, y_slab) + [y_slab(h, 4, 0, yy1, up), y_slab(h, 5, 1, yy2, dn)]:
+                cp.wait_send()
+
+        @pl.when((c == 1) & (z == h))
+        def _():
+            for n, yy in ((0, y), (1, yy1), (2, yy2), (3, yy3)):
+                z_arrived(h, n, yy)
+                project(0, yy)
+                project(1, yy)
+
+        z_left(h, 0, y, o.at[h])
+
+        @pl.when(c == 1)
+        def _():
+            for n, yy in ((1, yy1), (2, yy2), (3, yy3)):
+                z_left(h, n, yy, ybuf.at[yy, h])
+            for cp in y_own(h, y_part, first=True):
+                cp.wait_send()
+            y_part(h, 4, 0, yy1, up).wait_send()
+            y_part(h, 5, 1, yy2, dn).wait_send()
+
     def step(t, _):
         @pl.when(t == 8)
         def _():
@@ -382,12 +540,36 @@
         rows = pl.ds(pl.multiple_of(j * GROUP, GROUP), GROUP)
         st = absorb(qh, rows, dot_nt(q[qh, rows, :], kc[...]), lambda: vc[...])
         settle(qh, rows, st)
-        o_ref[qh, rows, :] = (
+        o[qh, rows, :] = (
             acc[qh, rows, :] / jnp.sum(l_s[qh, rows, :], axis=-1, keepdims=True)
         ).astype(jnp.bfloat16)
         return 0
 
-    lax.fori_loop(0, 8, mem_group, 0)
+    lax.fori_loop(0, 4, mem_group, 0)
+    heads_start(0)
+    lax.fori_loop(4, 8, mem_group, 0)
+    heads_start(1)
+
+    def wait_w(i, _):
+        @pl.when(i != hd)
+        def _():
+            rows = pl.ds(pl.multiple_of(i * 256, 256), 256)
+            remote(
+                w_hbm.at[:, pl.ds(0, 512)], wc.at[rows, :], w_send.at[i], w_recv.at[i], (sib, hd)
+            ).wait_recv()
+        return 0
+
+    lax.fori_loop(0, 8, wait_w, 0)
+    w_local.wait()
+    total[...] = jnp.zeros_like(total)
+    heads_mid(0)
+    heads_mid(1)
+    heads_near(0)
+    heads_near(1)
+    heads_fwd(0)
+    heads_fwd(1)
+    heads_end(0)
+    heads_end(1)
 
     for cp in swaps:
         cp.wait_send()
@@ -421,14 +603,10 @@
         @pl.when(i != hd)
         def _():
             w_copy(i).wait_send()
-            rows = pl.ds(pl.multiple_of(i * 256, 256), 256)
-            remote(
-                w_hbm.at[:, pl.ds(0, 512)], wc_hbm.at[rows, :], w_send.at[i], w_recv.at[i], (sib, hd)
-            ).wait_recv()
         return 0
 
     lax.fori_loop(0, 8, drain_w, 0)
-    w_local.wait()
+    out_ref[...] = total[...].astype(jnp.bfloat16)
 
 
 def attention(q, k, v, mk, mv, req, info, w):
@@ -438,12 +616,9 @@
     dma = pltpu.SemaphoreType.DMA
     return pl.pallas_call(
         attention_kernel,
-        out_shape=(
-            jax.ShapeDtypeStruct((2, ROWS, HD), b16),
-            jax.ShapeDtypeStruct((2048, 512), b16),
-        ),
+        out_shape=jax.ShapeDtypeStruct((ROWS, 512), b16),
         in_specs=[any_] * 5 + [vm, vm, any_],
-        out_specs=(vm, any_),
+        out_specs=vm,
         scratch_shapes=[
             pltpu.VMEM((2, ROWS, HD), b16),
             pltpu.VMEM((16, 2, ROWS, HD), b16),
@@ -457,6 +632,11 @@
             pltpu.VMEM((8, 2, BLOCK, HD), b16),
             pltpu.VMEM((TOPB * BLOCK, HD), b16),
             pltpu.VMEM((TOPB * BLOCK, HD), b16),
+            pltpu.VMEM((2, ROWS, HD), b16),
+            pltpu.VMEM((4, 2, ROWS, HD), b16),
+            pltpu.VMEM((ROWS, 2048), b16),
+            pltpu.VMEM((2048, 512), b16),
+            pltpu.VMEM((ROWS, 512), jnp.float32),
             pltpu.VMEM((16, 8, 128), jnp.int32),
             pltpu.VMEM((8, 128), jnp.int32),
             pltpu.SMEM((16, 8, 128), jnp.int32),
@@ -475,148 +655,17 @@
             dma((2,)),
             dma((8,)),
             dma((8,)),
+            dma((16,)),
+            dma((32,)),
+            dma((12,)),
+            dma((16,)),
+            dma((8,)),
         ],
         compiler_params=pltpu.CompilerParams(
             collective_id=0, has_side_effects=True, vmem_limit_bytes=56 << 20
         ),
         name="attention",
     )(q, k, v, mk, mv, req, info, w)
-
-
-def gather_kernel(o_ref, a_ref, ybuf, send, recv, ysend, yrecv, loc_sem):
-    s, hd, z, x, c, zh, y = where_am_i()
-    up = zh * 4 + lax.rem(y + 1, 4)
-    dn = zh * 4 + lax.rem(y + 3, 4)
-    y1 = lax.rem(y + 3, 4)
-    y2 = lax.rem(y + 1, 4)
-    y3 = lax.rem(y + 2, 4)
-    peers = [(1 - z, zh), (1 - z, 1 - zh), (z, 1 - zh)]
-    bar = pltpu.get_barrier_semaphore()
-    for zd, zhd in peers:
-        pl.semaphore_signal(
-            bar, inc=1, device_id=(seq_of(zd, x, c), zhd * 4 + y), device_id_type=MESH
-        )
-    pl.semaphore_signal(bar, inc=1, device_id=(s, up), device_id_type=MESH)
-    pl.semaphore_signal(bar, inc=1, device_id=(s, dn), device_id_type=MESH)
-    pl.semaphore_wait(bar, 5)
-
-    def head_cols(zhs, ys, zs):
-        return pl.ds(pl.multiple_of(((zhs * 4 + ys) * 2 + zs) * HD, HD), HD)
-
-    def z_send(src, ys, p, n):
-        zd, zhd = peers[p]
-        return remote(
-            src(zd), a_ref.at[:, head_cols(zh, ys, z)], send.at[n * 3 + p], recv.at[n * 3 + p],
-            (seq_of(zd, x, c), zhd * 4 + y),
-        )
-
-    def z_wait(ys, p, n):
-        zd, zhd = peers[p]
-        remote(
-            o_ref.at[0], a_ref.at[:, head_cols(zhd, ys, zd)], send.at[n * 3 + p],
-            recv.at[n * 3 + p], (s, hd),
-        ).wait_recv()
-
-    own = pltpu.make_async_copy(o_ref.at[z], a_ref.at[:, head_cols(zh, y, z)], loc_sem.at[0])
-    own.start()
-    outs = [z_send(lambda zd: o_ref.at[zd], y, p, 0) for p in range(3)]
-
-    @pl.when(c == 0)
-    def _():
-        for cp in outs:
-            cp.start()
-        own.wait()
-        for p in range(3):
-            z_wait(y, p, 0)
-
-        def slab(zz, yy):
-            return a_ref.at[:, pl.ds(pl.multiple_of((zz * 4 + yy) * 256, 256), 256)]
-
-        def y_copy(n, zz, yy, dev):
-            return remote(slab(zz, yy), slab(zz, yy), ysend.at[n], yrecv.at[yy * 2 + zz], (s, dev))
-
-        sends = [y_copy(0, 0, y, up), y_copy(1, 1, y, dn), y_copy(2, 1, y, up), y_copy(3, 0, y, dn)]
-        for cp in sends:
-            cp.start()
-        y_copy(0, 0, y1, up).wait_recv()
-        f0 = y_copy(4, 0, y1, up)
-        f0.start()
-        y_copy(0, 1, y2, up).wait_recv()
-        f1 = y_copy(5, 1, y2, dn)
-        f1.start()
-        for zz, yy in ((1, y1), (0, y2), (0, y3), (1, y3)):
-            y_copy(0, zz, yy, up).wait_recv()
-        for cp in outs + sends + [f0, f1]:
-            cp.wait_send()
-
-    @pl.when(c == 1)
-    def _():
-        def y_copy(n, h, yy, dev, first=False):
-            src = o_ref.at[h] if first else ybuf.at[yy, h]
-            return remote(src, ybuf.at[yy, h], ysend.at[n], yrecv.at[yy * 2 + h], (s, dev))
-
-        sends = [
-            y_copy(0, 0, y, up, True), y_copy(1, 1, y, dn, True),
-            y_copy(2, 1, y, up, True), y_copy(3, 0, y, dn, True),
-        ]
-        for cp in sends:
-            cp.start()
-        for cp in outs:
-            cp.start()
-        y_copy(0, 0, y1, up).wait_recv()
-        f0 = y_copy(4, 0, y1, up)
-        f0.start()
-        y_copy(0, 1, y2, up).wait_recv()
-        f1 = y_copy(5, 1, y2, dn)
-        f1.start()
-        locs = []
-        more = []
-
-        def spread(yy, n):
-            cps = [z_send(lambda zd: ybuf.at[yy, zd], yy, p, n) for p in range(3)]
-            for cp in cps:
-                cp.start()
-            lc = pltpu.make_async_copy(
-                ybuf.at[yy, z], a_ref.at[:, head_cols(zh, yy, z)], loc_sem.at[n]
-            )
-            lc.start()
-            more.extend(cps)
-            locs.append(lc)
-
-        y_copy(0, 1, y1, up).wait_recv()
-        spread(y1, 1)
-        y_copy(0, 0, y2, up).wait_recv()
-        spread(y2, 2)
-        y_copy(0, 0, y3, up).wait_recv()
-        y_copy(0, 1, y3, up).wait_recv()
-        spread(y3, 3)
-        own.wait()
-        for lc in locs:
-            lc.wait()
-        for n, yy in enumerate((y, y1, y2, y3)):
-            for p in range(3):
-                z_wait(yy, p, n)
-        for cp in outs + sends + more + [f0, f1]:
-            cp.wait_send()
-
-
-def gather(o):
-    dma = pltpu.SemaphoreType.DMA
-    vm = pl.BlockSpec(memory_space=pltpu.VMEM)
-    return pl.pallas_call(
-        gather_kernel,
-        out_shape=jax.ShapeDtypeStruct((ROWS, 2048), jnp.bfloat16),
-        in_specs=[vm],
-        out_specs=vm,
-        scratch_shapes=[
-            pltpu.VMEM((4, 2, ROWS, HD), jnp.bfloat16),
-            dma((12,)), dma((12,)), dma((6,)), dma((8,)), dma((4,)),
-        ],
-        compiler_params=pltpu.CompilerParams(
-            collective_id=1, has_side_effects=True, vmem_limit_bytes=32 << 20
-        ),
-        name="gather_heads",
-    )(o)
 
 
 def tables(block_index):
@@ -656,11 +705,9 @@
 
 def shards(q, k, v, mk, mv, block_index, w):
     req, info = tables(block_index)
-    o, wc = attention(
+    return attention(
         q, k, v, mk.reshape(-1, BLOCK, 2 * HD), mv.reshape(-1, BLOCK, 2 * HD), req, info, w
     )
-    a = gather(o)
-    return jnp.dot(a, wc, preferred_element_type=jnp.float32).astype(jnp.bfloat16)
 
 
 def solution(mesh):

time: 127 us -> 123 us (0.969)
  matrix products: 3.29 us -> 0 us
  Pallas kernels: 120 us -> 117 us
    dot_general x1 -> x0, matrix products: 3.29 us -> none  [shards(): jnp.dot(a, wc, preferred_element_type=jnp.float32).astype(jnp.bfloat16)]
    pallas_call x2 -> x1, Pallas kernels: 120 us -> 117 us  [attention(): pl.pallas_call(attention_kernel, out_shape=jax.ShapeDtypeStruct((ROWS, 51...]
where the time goes in v4:
time: 123 us; the launch traced here: 122 us
  Pallas kernels  117 us (95%)
  local copies, waits for them, and re-layouts  4.26 us (3%)
    pallas_call x1, Pallas kernels, attention(): pl.pallas_call(attention_kernel, out_shape=jax.ShapeDtypeStruct((ROWS, 51...  117 us

profile of v4, /device:TPU:0, one launch (start us, length us, event | category | flops | bytes accessed | tf_op | source)
XLA Modules:
  0.0 122.4 jit_solution(13315015092425204516)
XLA Ops:
  0.0 0.8 reshape.234
  0.8 0.2 fusion
  1.0 0.1 add_reduce_fusion
  1.1 0.1 iota_compare_fusion.4
  1.2 0.6 broadcast_in_dim.77.info_ref
  1.8 0.1 iota_compare_fusion.2
  1.9 0.2 select_reduce_fusion
  2.1 0.6 broadcast_in_dim.42.req_ref
  2.7 117.4 %attention.1 = bf16[1024,512]{1,0:T(8,128)(2,1)} custom-call(bf16[1024,256]{1,0:T(8,128)(2,1)} %q_hbm.1, bf16[1024,256]{1,0:T(8,128)(2,1)} %k_hbm.1, bf16[1024,256]{1,0:T(8,128)(2,1)} %v_hbm.1, bf16[64,64,256]{2,1,0:T(8,128)(2,1)} %bitcast.2, bf16[64,64,256]{2,1,0:T(8,128)(2,1)} %bitcast.3, s32[16,8,128]{2,1,0:T(8,128)} %broadcast_in_dim.42.req_ref, ...), custom_call_target="tpu_custom_call" | custom-call | tf_op jit(solution)/shard_map/attention/pallas_call | solution.py:617
  120.1 2.3 %copy.9 = bf16[1024,512]{1,0:T(8,128)(2,1)} copy(bf16[1024,512]{1,0:T(8,128)(2,1)} %attention.1) | data formatting | bytes 2097152
  (5 shorter events, 0.0 us)

commit v5 on v4

--- a/solution.py
+++ b/solution.py
@@ -530,24 +530,35 @@
     for j in range(8):
         mem[64 + j] = hot[j]
 
-    def mem_group(i, _):
-        qh = i // 4
-        j = lax.rem(i, 4)
-        for e in range(TOPB):
-            code = infos[qh, 0, j * TOPB + e]
-            kc[e * BLOCK:(e + 1) * BLOCK, :] = mem[code, 0]
-            vc[e * BLOCK:(e + 1) * BLOCK, :] = mem[code, 1]
-        rows = pl.ds(pl.multiple_of(j * GROUP, GROUP), GROUP)
-        st = absorb(qh, rows, dot_nt(q[qh, rows, :], kc[...]), lambda: vc[...])
-        settle(qh, rows, st)
-        o[qh, rows, :] = (
-            acc[qh, rows, :] / jnp.sum(l_s[qh, rows, :], axis=-1, keepdims=True)
-        ).astype(jnp.bfloat16)
-        return 0
-
-    lax.fori_loop(0, 4, mem_group, 0)
+    def mem_groups(i, _):
+        qh = i // 2
+        for b2 in range(2):
+            j = lax.rem(i, 2) * 2 + b2
+            for e in range(TOPB):
+                code = infos[qh, 0, j * TOPB + e]
+                kc[b2, e * BLOCK:(e + 1) * BLOCK, :] = mem[code, 0]
+                vc[b2, e * BLOCK:(e + 1) * BLOCK, :] = mem[code, 1]
+
+        def rows_of(b2):
+            return pl.ds(pl.multiple_of((lax.rem(i, 2) * 2 + b2) * GROUP, GROUP), GROUP)
+
+        def scores(b2):
+            rows = rows_of(b2)
+            return absorb(qh, rows, dot_nt(q[qh, rows, :], kc[b2]), lambda: vc[b2])
+
+        def finish(b2, st):
+            rows = rows_of(b2)
+            settle(qh, rows, st)
+            o[qh, rows, :] = (
+                acc[qh, rows, :] / jnp.sum(l_s[qh, rows, :], axis=-1, keepdims=True)
+            ).astype(jnp.bfloat16)
+
+        pipelined(2, scores, finish)
+        return 0
+
+    lax.fori_loop(0, 2, mem_groups, 0)
     heads_start(0)
-    lax.fori_loop(4, 8, mem_group, 0)
+    lax.fori_loop(2, 4, mem_groups, 0)
     heads_start(1)
 
     def wait_w(i, _):
@@ -630,8 +641,8 @@
             pltpu.VMEM((16, 2, 2, 2, BLOCK, HD), b16),
             pltpu.VMEM((72, 2, BLOCK, HD), b16),
             pltpu.VMEM((8, 2, BLOCK, HD), b16),
-            pltpu.VMEM((TOPB * BLOCK, HD), b16),
-            pltpu.VMEM((TOPB * BLOCK, HD), b16),
+            pltpu.VMEM((2, TOPB * BLOCK, HD), b16),
+            pltpu.VMEM((2, TOPB * BLOCK, HD), b16),
             pltpu.VMEM((2, ROWS, HD), b16),
             pltpu.VMEM((4, 2, ROWS, HD), b16),
             pltpu.VMEM((ROWS, 2048), b16),

time: 123 us -> 122 us (level)
  no operation moved by 1% of the time
where the time goes in v5:
time: 122 us
  Pallas kernels  117 us (96%)
  local copies, waits for them, and re-layouts  4.26 us (3%)
    pallas_call x1, Pallas kernels, attention(): pl.pallas_call(attention_kernel, out_shape=jax.ShapeDtypeStruct((ROWS, 51...  117 us

profile of v5, /device:TPU:0, one launch (start us, length us, event | category | flops | bytes accessed | tf_op | source)
XLA Modules:
  0.0 121.9 jit_solution(7397747586486700203)
XLA Ops:
  0.0 0.8 reshape.234
  0.8 0.2 fusion
  1.0 0.1 add_reduce_fusion
  1.1 0.1 iota_compare_fusion.4
  1.2 0.6 broadcast_in_dim.77.info_ref
  1.8 0.1 iota_compare_fusion.2
  1.9 0.2 select_reduce_fusion
  2.1 0.6 broadcast_in_dim.42.req_ref
  2.7 116.9 %attention.1 = bf16[1024,512]{1,0:T(8,128)(2,1)} custom-call(bf16[1024,256]{1,0:T(8,128)(2,1)} %q_hbm.1, bf16[1024,256]{1,0:T(8,128)(2,1)} %k_hbm.1, bf16[1024,256]{1,0:T(8,128)(2,1)} %v_hbm.1, bf16[64,64,256]{2,1,0:T(8,128)(2,1)} %bitcast.2, bf16[64,64,256]{2,1,0:T(8,128)(2,1)} %bitcast.3, s32[16,8,128]{2,1,0:T(8,128)} %broadcast_in_dim.42.req_ref, ...), custom_call_target="tpu_custom_call" | custom-call | tf_op jit(solution)/shard_map/attention/pallas_call | solution.py:628
  119.6 2.3 %copy.9 = bf16[1024,512]{1,0:T(8,128)(2,1)} copy(bf16[1024,512]{1,0:T(8,128)(2,1)} %attention.1) | data formatting | bytes 2097152
  (5 shorter events, 0.0 us)
